TPU v7x, 256 devices: a whole 4x4x8 slice. The times are simulated.
256 devices in a mesh: rows: 32 (over y, z), cols: 8 (over x, core).
Axes of the slice: x: 4, y: 4, z: 8, core: 2. Of those that a mesh axis runs over, the one named last changes fastest.
Arguments:
- samples: float32 [128, 131072], P('cols', 'rows')
- loadings: bfloat16 [256, 131072], P(None, 'rows')
- omega_tiles: float32 [1280, 512, 512], P(('rows', 'cols')), may hold values from -0.18 to 0.18
- omega_diagonal: float32 [131072], P('rows'), may hold values from 0.5 to 2
- tile_rows: int32 [1280], replicated, may hold values from 0 to 255, as said below
- tile_cols: int32 [1280], replicated, may hold values from 0 to 255, as said below
Outputs:
- new_tiles: float32 [1280, 512, 512], P(('rows', 'cols'))
- new_diagonal: float32 [131072], P('rows')
Inputs may be any that keep to these rules, and one draw needn't show every extreme that they name: Slot s belongs to group g = s // 40; tile_rows[s] lies between g * 8 and g * 8 + 7. A block row may hold any number of tiles, none included. `tile_cols`: of the 40 tiles of one group, at most 3 have column blocks in any one group h (blocks h * 8 to h * 8 + 7), and in every group exactly 3 have column blocks in some one group.
All inputs are finite; a program needn't handle non-finite values.
Results may differ from a plain program's by a relative error of at most 0.0003.
Values sent between devices are 32-bit elements; how exact they have to be, the bound alone decides.
A program may use at most 64 MiB of HBM per device.

v0:
```python
import jax
import jax.numpy as jnp
from jax import lax
from jax.sharding import PartitionSpec as P

step_size = 0.5
penalty = 0.02


def per_device(samples, loadings, omega_tiles, omega_diagonal, tile_rows, tile_cols):
    highest = lax.Precision.HIGHEST
    row_count = lax.axis_size("rows")
    col_count = lax.axis_size("cols")
    my_row = lax.axis_index("rows")
    my_col = lax.axis_index("cols")
    sample_dev, var_dev = samples.shape
    tile_dev = omega_tiles.shape[0]
    block_size = omega_tiles.shape[1]
    blocks_dev = var_dev // block_size
    group_tiles = tile_dev * col_count
    capacity = (2 * group_tiles + row_count - 1) // row_count
    sample_all = sample_dev * col_count
    factor_load = loadings.astype(jnp.float32)
    score_terms = lax.dot_general(
        samples,
        factor_load,
        (((1,), (1,)), ((), ())),
        precision=highest,
        preferred_element_type=jnp.float32,
    )
    shares = lax.psum_scatter(score_terms, "rows", scatter_dimension=1, tiled=True)
    scores = lax.all_gather(shares, "rows", axis=1, tiled=True)
    residual = samples - jnp.dot(
        scores, factor_load, precision=highest, preferred_element_type=jnp.float32
    )
    group_rows = tile_rows.reshape(row_count, group_tiles)
    group_cols = tile_cols.reshape(row_count, group_tiles)
    source_group = group_cols // blocks_dev
    source_local = group_cols % blocks_dev
    positions = jnp.arange(group_tiles)
    earlier = positions[None, :] < positions[:, None]
    same_group = source_group[:, :, None] == source_group[:, None, :]
    slot_rank = jnp.sum(same_group & earlier[None], axis=2)
    slot_ids = jnp.arange(capacity)
    chosen = (source_group[:, None, :] == my_row) & (
        slot_rank[:, None, :] == slot_ids[None, :, None]
    )
    pick_local = jnp.sum(jnp.where(chosen, source_local[:, None, :], 0), axis=2).reshape(-1)
    pick_live = jnp.any(chosen, axis=2).reshape(-1)
    own_group = lax.dynamic_index_in_dim(source_group, my_row, 0, keepdims=False)
    own_rank = lax.dynamic_index_in_dim(slot_rank, my_row, 0, keepdims=False)
    forward_index = own_group * capacity + own_rank
    group_row_ids = lax.dynamic_index_in_dim(group_rows, my_row, 0, keepdims=False)
    group_col_ids = lax.dynamic_index_in_dim(group_cols, my_row, 0, keepdims=False)
    mine_rows = (
        lax.dynamic_slice_in_dim(group_row_ids, my_col * tile_dev, tile_dev) - my_row * blocks_dev
    )
    mine_cols = lax.dynamic_slice_in_dim(group_col_ids, my_col * tile_dev, tile_dev)
    mine_is_diag = mine_rows + my_row * blocks_dev == mine_cols

    def outbound(field_in):
        blocks = field_in.reshape(sample_dev, blocks_dev, block_size)
        picked = jnp.take(blocks, pick_local, axis=1)
        picked = jnp.where(pick_live[None, :, None], picked, 0.0)
        return picked.reshape(sample_dev, row_count, capacity, block_size)

    def forward(arrived):
        flattened = arrived.reshape(sample_dev, row_count * capacity, block_size)
        return jnp.take(flattened, forward_index, axis=1).reshape(
            sample_dev, col_count, tile_dev, block_size
        )

    arrived_resid = lax.all_to_all(
        outbound(residual), "rows", split_axis=1, concat_axis=1, tiled=True
    )
    routed_resid = lax.all_to_all(
        forward(arrived_resid), "cols", split_axis=1, concat_axis=0, tiled=True
    ).reshape(sample_all, tile_dev, block_size)
    resid_group = lax.all_gather(residual, "cols", axis=0, tiled=True)
    diagonal_mask = jnp.arange(block_size)[:, None] == jnp.arange(block_size)[None, :]
    keep_mask = jnp.where(mine_is_diag[:, None, None] & diagonal_mask[None], 0.0, 1.0)
    tiles_kept = omega_tiles * keep_mask
    products = jnp.einsum(
        "skb,kab->ska",
        routed_resid,
        tiles_kept,
        precision=highest,
        preferred_element_type=jnp.float32,
    )
    placement = (mine_rows[:, None] == jnp.arange(blocks_dev)[None, :]).astype(jnp.float32)
    partial_y = jnp.einsum(
        "ska,kr->sra", products, placement, precision=highest, preferred_element_type=jnp.float32
    ).reshape(sample_all, var_dev)
    applied = (
        lax.psum_scatter(partial_y, "cols", scatter_dimension=0, tiled=True)
        + omega_diagonal * residual
    )
    applied_group = lax.all_gather(applied, "cols", axis=0, tiled=True)
    arrived_applied = lax.all_to_all(
        outbound(applied), "rows", split_axis=1, concat_axis=1, tiled=True
    )
    routed_applied = lax.all_to_all(
        forward(arrived_applied), "cols", split_axis=1, concat_axis=0, tiled=True
    ).reshape(sample_all, tile_dev, block_size)
    row_resid = jnp.take(resid_group.reshape(sample_all, blocks_dev, block_size), mine_rows, axis=1)
    row_applied = jnp.take(
        applied_group.reshape(sample_all, blocks_dev, block_size), mine_rows, axis=1
    )
    first_term = jnp.einsum(
        "ska,skb->kab",
        row_applied,
        routed_resid,
        precision=highest,
        preferred_element_type=jnp.float32,
    )
    second = jnp.einsum(
        "ska,skb->kab",
        row_resid,
        routed_applied,
        precision=highest,
        preferred_element_type=jnp.float32,
    )
    gradient = 0.5 * (first_term + second) / sample_all
    stepped = (omega_tiles - step_size * gradient) * keep_mask
    new_tiles = jnp.sign(stepped) * jnp.maximum(jnp.abs(stepped) - step_size * penalty, 0.0)
    diag_stat = jnp.sum(applied_group * resid_group, axis=0) / sample_all
    new_diagonal = omega_diagonal - step_size * (diag_stat - 1.0 / omega_diagonal)
    return (new_tiles, new_diagonal)


def solution(mesh):
    placed = (
        P("cols", "rows"),
        P(None, "rows"),
        P(("rows", "cols"), None, None),
        P("rows"),
        P(),
        P(),
    )
    return jax.shard_map(
        per_device,
        mesh=mesh,
        in_specs=placed,
        out_specs=(P(("rows", "cols"), None, None), P("rows")),
        check_vma=False,
    )
```

profile of v0, /device:TPU:1, one launch (start us, length us, event | category | flops | bytes accessed | tf_op | source)
XLA Modules:
  0.0 478.2 jit_solution(12511604730167922913)
XLA Ops:
  9.8 2.7 fusion.27
  12.5 118.9 %all-reduce = f32[16,256]{1,0:T(8,128)S(1)} all-reduce(f32[16,256]{1,0:T(8,128)S(1)} %fusion.27), channel_id=2, replica_groups=mesh['rows'=32,'cols'=8] {'rows'}, use_global_device_ids=true, to_apply=%region_2.3.clone | all-reduce | flops 4096 | bytes 32768
  132.8 30.8 %all_gather.9 = f32[16,256]{0,1:T(8,128)S(1)} all-gather(f32[16,8]{0,1:T(8,128)S(1)} %copy.30), channel_id=1, replica_groups=mesh['rows'=32,'cols'=8] {'rows'}, dimensions={1}, use_global_device_ids=true | all-gather | bytes 16896 | tf_op jit(solution)/shard_map/all_gather | solution.py:32
  167.0 3.9 bitcast_select_fusion.1
  170.9 5.5 %all-to-all-start = ((f32[16,32,3,512]{3,0,2,1:T(8,128)}), f32[16,32,3,512]{3,0,2,1:T(8,128)}, u32[]{:S(2)}, u32[]{:S(2)}) async-start(f32[16,32,3,512]{3,0,2,1:T(8,128)} %bitcast.73), calls=%async_computation | async-start | bytes 6291456 | tf_op jit(solution)/shard_map/all_to_all | solution.py:73
  176.5 40.0 %all-to-all-done = f32[16,32,3,512]{3,0,2,1:T(8,128)} async-done(((f32[16,32,3,512]{3,0,2,1:T(8,128)}), f32[16,32,3,512]{3,0,2,1:T(8,128)}, u32[]{:S(2)}, u32[]{:S(2)}) %all-to-all-start) | async-done | bytes 3145760 | tf_op jit(solution)/shard_map/all_to_all | solution.py:73
  216.4 2.5 gather_fusion.1
  220.2 53.5 %all-to-all-start.1 = ((f32[16,8,5,512]{3,0,2,1:T(8,128)}), f32[16,8,5,512]{3,0,2,1:T(8,128)S(1)}, u32[]{:S(2)}, u32[]{:S(2)}) async-start(f32[16,8,5,512]{3,0,2,1:T(8,128)} %bitcast.8), calls=%async_computation.1 | async-start | bytes 2621440 | tf_op jit(solution)/shard_map/all_to_all | solution.py:76
  274.0 17.5 %all-to-all-done.1 = f32[16,8,5,512]{3,0,2,1:T(8,128)S(1)} async-done(((f32[16,8,5,512]{3,0,2,1:T(8,128)}), f32[16,8,5,512]{3,0,2,1:T(8,128)S(1)}, u32[]{:S(2)}, u32[]{:S(2)}) %all-to-all-start.1) | async-done | bytes 1310752 | tf_op jit(solution)/shard_map/all_to_all | solution.py:76
  291.7 7.3 %fusion.5 = f32[128,5,512]{0,2,1:T(8,128)S(1)} fusion(f32[128,5,512]{2,0,1:T(8,128)S(1)} %bitcast.75, f32[5,512,512]{2,1,0:T(8,128)} %param.14, pred[512,512]{1,0:T(8,128)(4,1)S(1)} %iota_compare_fusion, pred[5]{0:T(512)(128)(4,1)S(1)} %compare_bitcast_fusion), kind=kOutput, calls=%fused_computation.20 | convolution fusion | flops 2017198080 | bytes 8126469 | tf_op jit(solution)/shard_map/skb,kab->ska/dot_general | solution.py:83
  300.9 2.6 fusion.20
  303.5 3.0 copy.49
  307.3 29.2 %reduce-scatter.3.cloned.1.call-done = f32[16,4096]{1,0:T(8,128)} async-done(((f32[128,4096]{1,0:T(8,128)}), f32[16,4096]{1,0:T(8,128)}) %reduce-scatter.3.cloned.1.call-update) | async-done | bytes 262160 | tf_op jit(solution)/shard_map/reduce_scatter | solution.py:95
  339.9 3.9 bitcast_select_fusion
  343.8 9.5 %all-to-all-start.2 = ((f32[16,32,3,512]{3,0,2,1:T(8,128)}), f32[16,32,3,512]{3,0,2,1:T(8,128)}, u32[]{:S(2)}, u32[]{:S(2)}) async-start(f32[16,32,3,512]{3,0,2,1:T(8,128)} %bitcast.74), calls=%async_computation.3 | async-start | bytes 6291456 | tf_op jit(solution)/shard_map/all_to_all | solution.py:99
  354.1 68.3 %all-to-all-done.2 = f32[16,32,3,512]{3,0,2,1:T(8,128)} async-done(((f32[16,32,3,512]{3,0,2,1:T(8,128)}), f32[16,32,3,512]{3,0,2,1:T(8,128)}, u32[]{:S(2)}, u32[]{:S(2)}) %all-to-all-start.2) | async-done | bytes 3145760 | tf_op jit(solution)/shard_map/all_to_all | solution.py:99
  422.4 2.5 gather_fusion.5
  426.1 10.7 %all-to-all-start.3 = ((f32[16,8,5,512]{3,0,2,1:T(8,128)}), f32[16,8,5,512]{3,0,2,1:T(8,128)}, u32[]{:S(2)}, u32[]{:S(2)}) async-start(f32[16,8,5,512]{3,0,2,1:T(8,128)} %bitcast.20), calls=%async_computation.4 | async-start | bytes 2621440 | tf_op jit(solution)/shard_map/all_to_all | solution.py:102
  436.8 3.1 copy.54
  442.2 3.1 copy.55
  445.4 3.4 gather_fusion.2
  448.8 2.6 multiply_reduce_fusion
  452.0 6.2 %fusion.7 = f32[5,512,512]{2,1,0:T(8,128)} fusion(f32[128,5,512]{2,0,1:T(8,128)S(1)} %bitcast.76, f32[5,128,512]{2,1,0:T(8,128)S(1)} %copy-done.2, pred[5]{0:T(512)(128)(4,1)S(1)} %get-tuple-element.4), kind=kOutput, calls=%fused_computation.22 | convolution fusion | flops 2013593600 | bytes 7864325 | tf_op jit(solution)/shard_map/ska,skb->kab/dot_general | solution.py:109
  459.7 12.0 %maximum_multiply_fusion = f32[5,512,512]{2,1,0:T(8,128)} fusion(f32[5,512,512]{2,1,0:T(8,128)} %param.14, f32[5,512,512]{2,1,0:T(8,128)} %fusion.7, pred[512,512]{1,0:T(8,128)(4,1)S(1)} %copy-done.6, pred[5]{0:T(512)(128)(4,1)S(1)} %compare_bitcast_fusion, f32[128,5,512]{2,0,1:T(8,128)S(1)} %bitcast.83, f32[5,128,512]{2,1,0:T(8,128)S(1)} %gather_fusion.3, ...), kind=kOutput, calls=%fused_computation.9 | convolution fusion | flops 2028011520 | bytes 18612234 | tf_op jit(solution)/shard_map/ska,skb->kab/dot_general | solution.py:116
  (71 shorter events, 20.8 us)
Async XLA Ops:
  7.2 2.6 copy-start
  7.2 124.2 %copy-start.11 = (u32[256]{0:T(256)S(1)}, u32[256]{0:T(256)}, u32[]{:S(2)}) copy-start(u32[256]{0:T(256)} %constant.133) | copy-start | bytes 3076
  7.2 156.4 %copy-start.8 = (f32[16,4096]{1,0:T(8,128)S(1)}, f32[16,4096]{1,0:T(8,128)}, u32[]{:S(2)}) copy-start(f32[16,4096]{1,0:T(8,128)} %param.12) | copy-start | bytes 786436
  164.5 2.4 copy-start.3
  170.9 45.5 %all-to-all-start = ((f32[16,32,3,512]{3,0,2,1:T(8,128)}), f32[16,32,3,512]{3,0,2,1:T(8,128)}, u32[]{:S(2)}, u32[]{:S(2)}) async-start(f32[16,32,3,512]{3,0,2,1:T(8,128)} %bitcast.73), calls=%async_computation | async-start | bytes 6291456 | tf_op jit(solution)/shard_map/all_to_all | solution.py:73
  219.0 54.7 %copy-start.10 = (s32[1280]{0:T(1024)S(1)}, s32[1280]{0:T(1024)}, u32[]{:S(2)}) copy-start(s32[1280]{0:T(1024)} %param.16) | copy-start | bytes 15364
  220.2 71.4 %all-to-all-start.1 = ((f32[16,8,5,512]{3,0,2,1:T(8,128)}), f32[16,8,5,512]{3,0,2,1:T(8,128)S(1)}, u32[]{:S(2)}, u32[]{:S(2)}) async-start(f32[16,8,5,512]{3,0,2,1:T(8,128)} %bitcast.8), calls=%async_computation.1 | async-start | bytes 2621440 | tf_op jit(solution)/shard_map/all_to_all | solution.py:76
  273.6 62.8 %reduce-scatter.3.cloned.1.call-start = ((), (), s32[]{:S(2)}) async-start(), calls=%async_computation.5 | async-start | bytes 2359296 | tf_op jit(solution)/shard_map/reduce_scatter | solution.py:95
  274.0 24.9 %copy-start.5 = (pred[512,512]{1,0:T(8,128)(4,1)}, pred[512,512]{1,0:T(8,128)(4,1)S(1)}, u32[]{:S(2)}) copy-start(pred[512,512]{1,0:T(8,128)(4,1)S(1)} %iota_compare_fusion) | copy-start | bytes 786436
  306.5 30.0 %copy-start.4 = (f32[16,4096]{1,0:T(8,128)S(1)}, f32[16,4096]{1,0:T(8,128)}, u32[]{:S(2)}) copy-start(f32[16,4096]{1,0:T(8,128)} %copy-done.3) | copy-start | bytes 786436
  306.5 30.0 %copy-start.9 = (f32[4096]{0:T(1024)S(1)}, f32[4096]{0:T(1024)}, u32[]{:S(2)}) copy-start(f32[4096]{0:T(1024)} %param.15) | copy-start | bytes 49156
  306.5 130.3 %all-gather.5.cloned.1.call-start = ((), (), s32[]{:S(2)}) async-start(), calls=%async_computation.7 | async-start | bytes 2359296 | tf_op jit(solution)/shard_map/all_gather | solution.py:79
  337.4 2.5 copy-start.7
  343.8 78.6 %all-to-all-start.2 = ((f32[16,32,3,512]{3,0,2,1:T(8,128)}), f32[16,32,3,512]{3,0,2,1:T(8,128)}, u32[]{:S(2)}, u32[]{:S(2)}) async-start(f32[16,32,3,512]{3,0,2,1:T(8,128)} %bitcast.74), calls=%async_computation.3 | async-start | bytes 6291456 | tf_op jit(solution)/shard_map/all_to_all | solution.py:99
  353.4 88.9 %all-gather.3.cloned.1.call-start = ((), (), s32[]{:S(2)}) async-start(), calls=%async_computation.6 | async-start | bytes 2359296 | tf_op jit(solution)/shard_map/all_gather | solution.py:98
  426.1 32.1 %all-to-all-start.3 = ((f32[16,8,5,512]{3,0,2,1:T(8,128)}), f32[16,8,5,512]{3,0,2,1:T(8,128)}, u32[]{:S(2)}, u32[]{:S(2)}) async-start(f32[16,8,5,512]{3,0,2,1:T(8,128)} %bitcast.20), calls=%async_computation.4 | async-start | bytes 2621440 | tf_op jit(solution)/shard_map/all_to_all | solution.py:102
  448.8 3.2 copy-start.2
  458.2 1.5 copy-start.6
  459.7 12.0 %copy-start.1 = (bf16[256,4096]{1,0:T(8,128)(2,1)S(1)}, bf16[256,4096]{1,0:T(8,128)(2,1)}, u32[]{:S(2)}) copy-start(bf16[256,4096]{1,0:T(8,128)(2,1)} %param.13) | copy-start | bytes 6291460
Sparse Core Ops, SparseCore 0:
  306.6 29.7 reduce-scatter.2
  338.3 29.6 all-gather.4
  369.8 28.0 all-gather.2
where the time goes:
time: 479 us; the launch traced here: 478 us
  waiting for transfers between devices  156 us (33%)
  blocking collectives  150 us (31%)
  starting transfers between devices  79.4 us (17%)
  matrix products  31.8 us (7%)
  local copies, waits for them, and re-layouts  30.5 us (6%)
  other arithmetic  15.9 us (3%)
  between operations  14.7 us (3%)
    unnamed x1, blocking collectives  119 us
    all_to_all x1, waiting for transfers between devices, per_device(): lax.all_to_all(outbound(applied), 'rows', split_axis=1, concat_axis=1, ti...  68.3 us
    all_to_all x1, starting transfers between devices, per_device(): lax.all_to_all(forward(arrived_resid), 'cols', split_axis=1, concat_axis=...  53.5 us
    all_to_all x1, waiting for transfers between devices, per_device(): lax.all_to_all(outbound(residual), 'rows', split_axis=1, concat_axis=1, t...  40 us
    all_gather x1, blocking collectives, per_device(): scores = lax.all_gather(shares, 'rows', axis=1, tiled=True)  30.8 us
    reduce_scatter x1, waiting for transfers between devices, per_device(): lax.psum_scatter(partial_y, 'cols', scatter_dimension=0, tiled=True)  29.2 us
    all_to_all x1, waiting for transfers between devices, per_device(): lax.all_to_all(forward(arrived_resid), 'cols', split_axis=1, concat_axis=...  17.5 us
    dot_general x1, matrix products, per_device(): jnp.einsum('ska,skb->kab', row_resid, routed_applied, precision=highest,...  12 us
  transfers between devices with their start and end apart: 7, of which 4 were waited for; matrix products, arithmetic and copies ran while one was open for 7% of the time, Pallas kernels for 0%

commit v1 on v0

v1 whole, which is shorter than its diff:
```python
import functools
import jax
import jax.numpy as jnp
from jax import lax
from jax.experimental import pallas as pl
from jax.experimental.pallas import tpu as pltpu
from jax.sharding import PartitionSpec as P

step_size = 0.5
penalty = 0.02
MESH = pl.DeviceIdType.MESH
CAP = 3
Y = 4
Z = 8
C = 8
BLK = 8
TD = 5
NC = 2
SC = 8
BS = 512
PLANE = Z * BLK
SLOTS = Z * CAP

PICK = 0
FWD = PICK + (Y - 1) * SLOTS
ORDER = FWD + C * TD
SAME = ORDER + C * TD
LAST = SAME + C * TD
HAS = LAST + BLK
DIAG = HAS + BLK
META = DIAG + TD


def split2(x):
    hi = x.astype(jnp.bfloat16)
    return hi, (x - hi.astype(jnp.float32)).astype(jnp.bfloat16)


def split3(x):
    hi, rest = x.astype(jnp.bfloat16), None
    rest = x - hi.astype(jnp.float32)
    mid, low = split2(rest)
    return jnp.concatenate([hi, mid, low], axis=0)


def dot(a, b, dims):
    return lax.dot_general(a, b, (dims, ((), ())), preferred_element_type=jnp.float32)


def wait_all(ref, sem):
    pltpu.make_async_copy(ref, ref, sem).wait()


def route_kernel(
    meta,
    samples,
    loadings,
    diag,
    tiles,
    routed_out,
    group_out,
    diag_out,
    part,
    score_z,
    score_y,
    stage,
    seg,
    tile_f32,
    tile_hi,
    tile_lo,
    group,
    *rest,
):
    n = 2 * NC
    pair = lambda flat: (flat[:NC], flat[NC:])
    field, ysend, fsend, frecv = (pair(rest[i * n : (i + 1) * n]) for i in range(4))
    rest = rest[4 * n :]
    psend, precv = rest[:NC], rest[NC : 2 * NC]
    (
        exch_s,
        exch_r,
        ring_s,
        ring_r,
        y_s,
        y_r,
        f_s,
        f_r,
        p_s,
        p_r,
        g_s,
        g_r,
        local,
    ) = rest[2 * NC :]

    row = lax.axis_index("rows")
    me = lax.axis_index("cols")
    y, z = row // Z, row % Z
    at_z = lambda d: {"rows": y * Z + (z + d + Z) % Z}
    at_y = lambda d: {"rows": ((y + d) % Y) * Z + z}
    at_c = lambda d: {"cols": (me + d + C) % C}

    def remote(src, dst, send, recv, where):
        return pltpu.make_async_remote_copy(
            src_ref=src,
            dst_ref=dst,
            send_sem=send,
            recv_sem=recv,
            device_id=where,
            device_id_type=MESH,
        )

    def each(low, high, body):
        lax.fori_loop(low, high, lambda i, _: (body(i), None)[1], None)

    barrier = pltpu.get_barrier_semaphore()

    def greet(where, count):
        each(
            1,
            count,
            lambda d: pl.semaphore_signal(
                barrier, inc=1, device_id=where(d), device_id_type=MESH
            ),
        )

    greet(at_z, Z)
    greet(at_y, Y)
    greet(at_c, C)
    tile_copy = pltpu.make_async_copy(tiles, tile_f32, local.at[0])
    tile_copy.start()

    def score_step(b, total):
        cols = pl.ds(pl.multiple_of(b * BS, BS), BS)
        return total + dot(split3(samples[:, cols]), loadings[:, cols], ((1,), (1,)))

    ns = NC * SC
    total = lax.fori_loop(0, BLK, score_step, jnp.zeros((3 * ns, loadings.shape[0]), jnp.float32))
    part[0] = total[:ns] + total[ns : 2 * ns] + total[2 * ns :]
    pl.semaphore_wait(barrier, Z + Y + C - 3)

    each(
        1,
        Z,
        lambda d: remote(part.at[0], score_z.at[d], exch_s.at[0], exch_r.at[0], at_z(d)).start(),
    )
    wait_all(score_z.at[pl.ds(1, Z - 1)], exch_r.at[0])
    total = part[0]
    for d in range(1, Z):
        total = total + score_z[d]
    part[1] = total
    each(
        1,
        Y,
        lambda d: remote(part.at[1], score_y.at[d], exch_s.at[1], exch_r.at[1], at_y(d)).start(),
    )
    wait_all(score_y.at[pl.ds(1, Y - 1)], exch_r.at[1])
    for d in range(1, Y):
        total = total + score_y[d]
    scores = split3(total)

    def residual_step(b):
        cols = pl.ds(pl.multiple_of(b * BS, BS), BS)
        terms = dot(scores, loadings[:, cols], ((1,), (0,)))
        value = samples[:, cols] - (terms[:ns] + terms[ns : 2 * ns] + terms[2 * ns :])
        for h in range(NC):
            field[0][h][z * BLK + b] = value[h * SC : (h + 1) * SC]
            group[0, h, 0, b] = value[h * SC : (h + 1) * SC]

    each(0, BLK, residual_step)

    def hop(p, h, k, right):
        slice_of = ((z - k + 1 + Z) if right else (z + k - 1)) % Z
        ref = field[p][h]
        last = isinstance(k, int) and k == Z // 2
        low = slice_of * BLK + (0 if right or not last else BLK // 2)
        where = pl.ds(low, BLK // 2 if last else BLK)
        way = 0 if right else 1
        return remote(
            ref.at[where],
            ref.at[where],
            ring_s.at[p, h, way],
            ring_r.at[p, h, way, k],
            at_z(1 if right else -1),
        )

    def arrived(p, h, k, right):
        slice_of = ((z - k + Z) if right else (z + k)) % Z
        last = isinstance(k, int) and k == Z // 2
        low = slice_of * BLK + (0 if right or not last else BLK // 2)
        ref = field[p][h].at[pl.ds(low, BLK // 2 if last else BLK)]
        wait_all(ref, ring_r.at[p, h, 0 if right else 1, k])

    def send_picks(p, h, zs):
        ref = field[p][h]
        stage[...] = ref[pl.ds(zs * BLK, BLK)]

        def to_plane(i):
            base = i * SLOTS + zs * CAP
            for j in range(CAP):
                ysend[p][h][base + j] = stage[meta[PICK + base + j]]
            remote(
                ysend[p][h].at[pl.ds(base, CAP)],
                ref.at[pl.ds(PLANE + base, CAP)],
                y_s.at[p, h, i],
                y_r.at[p, h, i],
                at_y(i + 1),
            ).start()

        each(0, Y - 1, to_plane)

    def route(p, h, first=None, middle=None):
        hop(p, h, 1, True).start()
        hop(p, h, 1, False).start()
        send_picks(p, h, z)
        if first:
            first()

        def step(k):
            arrived(p, h, k, True)
            hop(p, h, k + 1, True).start()
            arrived(p, h, k, False)
            hop(p, h, k + 1, False).start()
            send_picks(p, h, (z - k + Z) % Z)
            send_picks(p, h, (z + k) % Z)

        each(1, Z // 2 - 1, step)
        step(Z // 2 - 1)
        if middle:
            middle()
        arrived(p, h, Z // 2, True)
        arrived(p, h, Z // 2, False)
        send_picks(p, h, (z + Z // 2) % Z)
        for i in range(Y - 1):
            wait_all(field[p][h].at[pl.ds(PLANE + i * SLOTS, SLOTS)], y_r.at[p, h, i])

    def forward(p, h):
        def one(d):
            dest = (me + d) % C
            for t in range(TD):
                fsend[p][h][d, t] = field[p][h][meta[FWD + dest * TD + t]]
            remote(
                fsend[p][h].at[d],
                frecv[p][h].at[d],
                f_s.at[p, h],
                f_r.at[p, h],
                at_c(d),
            ).start()

        each(1, C, one)
        for t in range(TD):
            frecv[p][h][0, t] = field[p][h][meta[FWD + me * TD + t]]

    def forwarded(p, h):
        wait_all(frecv[p][h].at[pl.ds(1, C - 1)], f_r.at[p, h])

    def gather_start(p, h):
        each(
            1,
            C,
            lambda d: remote(
                group.at[p, h, 0], group.at[p, h, d], g_s.at[p, h], g_r.at[p, h], at_c(d)
            ).start(),
        )

    def split_tiles():
        tile_copy.wait()
        rows = lax.broadcasted_iota(jnp.int32, (BS // 4, BS), 0)
        cols = lax.broadcasted_iota(jnp.int32, (BS // 4, BS), 1)

        def one(i):
            t, q = i // 4, i % 4
            at = pl.ds(pl.multiple_of(q * (BS // 4), BS // 4), BS // 4)
            flag = jnp.full((BS // 4, BS), meta[DIAG + t], jnp.int32)
            drop = (rows + q * (BS // 4) == cols) & (flag != 0)
            hi, lo = split2(jnp.where(drop, 0.0, tile_f32[t, at]))
            tile_hi[t, at] = hi
            tile_lo[t, at] = lo

        each(0, TD * 4, one)

    def products(h):
        forwarded(0, h)

        def one(t):
            hi, lo = split2(frecv[0][h][:, t].reshape(C * SC, BS))
            both = dot(jnp.concatenate([hi, lo], axis=0), tile_hi[t], ((1,), (1,)))
            value = both[: C * SC] + both[C * SC :] + dot(hi, tile_lo[t], ((1,), (1,)))
            value = value.reshape(C, SC, BS)
            for d in range(C):
                psend[h][d * TD + t] = value[d]

        each(0, TD, one)
        each(
            1,
            C,
            lambda d: remote(
                psend[h].at[pl.ds(d * TD, TD)],
                precv[h].at[pl.ds(d * TD, TD)],
                p_s.at[h],
                p_r.at[h],
                at_c(-d),
            ).start(),
        )
        for t in range(TD):
            precv[h][t] = psend[h][t]

    def apply_rows(h):
        wait_all(precv[h].at[pl.ds(TD, (C - 1) * TD)], p_r.at[h])

        def one(k, running):
            same = jnp.full((SC, BS), meta[SAME + k], jnp.int32) != 0
            running = jnp.where(same, running, 0.0) + precv[h][meta[ORDER + k]]
            seg[k] = running
            return running

        lax.fori_loop(0, C * TD, one, jnp.zeros((SC, BS), jnp.float32))

        def block(b):
            has = jnp.full((SC, BS), meta[HAS + b], jnp.int32) != 0
            value = jnp.where(has, seg[meta[LAST + b]], 0.0)
            value = value + diag[pl.ds(b, 1)] * group[0, h, 0, b]
            field[1][h][z * BLK + b] = value
            group[1, h, 0, b] = value

        each(0, BLK, block)

    def start_gathers():
        for h in range(NC):
            gather_start(0, h)

    route(0, 0, first=start_gathers, middle=split_tiles)
    forward(0, 0)
    route(0, 1, middle=lambda: products(0))
    forward(0, 1)
    apply_rows(0)
    route(1, 0, first=lambda: gather_start(1, 0), middle=lambda: products(1))
    forward(1, 0)
    apply_rows(1)
    route(1, 1, first=lambda: gather_start(1, 1))
    forward(1, 1)

    def out_copy(src, dst):
        copy = pltpu.make_async_copy(src, dst, local.at[1])
        copy.start()

    for p in range(2):
        for h in range(NC):
            wait_all(group.at[p, h, pl.ds(1, C - 1)], g_r.at[p, h])
    out_copy(group, group_out)

    def diag_step(b):
        total = jnp.zeros((SC, BS), jnp.float32)
        for h in range(NC):
            for d in range(C):
                total = total + group[0, h, d, b] * group[1, h, d, b]
        stat = jnp.sum(total, axis=0, keepdims=True) / (NC * C * SC)
        old = diag[pl.ds(b, 1)]
        diag_out[pl.ds(b, 1)] = old - step_size * (stat - 1.0 / old)

    each(0, BLK, diag_step)
    for p in range(2):
        for h in range(NC):
            if p == 1:
                forwarded(p, h)
            copy = pltpu.make_async_copy(frecv[p][h], routed_out.at[p, h], local.at[2 + p * NC + h])
            copy.start()

    wait_all(score_z.at[pl.ds(1, Z - 1)], exch_s.at[0])
    wait_all(score_y.at[pl.ds(1, Y - 1)], exch_s.at[1])
    sent = Z // 2 * BLK - BLK // 2
    for p in range(2):
        for h in range(NC):
            for way in range(2):
                wait_all(field[p][h].at[pl.ds(0, sent)], ring_s.at[p, h, way])
            for i in range(Y - 1):
                wait_all(ysend[p][h].at[pl.ds(i * SLOTS, SLOTS)], y_s.at[p, h, i])
            wait_all(fsend[p][h].at[pl.ds(1, C - 1)], f_s.at[p, h])
            wait_all(group.at[p, h, pl.ds(1, C - 1)], g_s.at[p, h])
    for h in range(NC):
        wait_all(psend[h].at[pl.ds(TD, (C - 1) * TD)], p_s.at[h])
    pltpu.make_async_copy(group, group_out, local.at[1]).wait()
    for p in range(2):
        for h in range(NC):
            pltpu.make_async_copy(
                frecv[p][h], routed_out.at[p, h], local.at[2 + p * NC + h]
            ).wait()


def step_kernel(info, routed, rows, tile, out):
    t = pl.program_id(0)
    samples = NC * C * SC
    flat = lambda ref, p: ref[p].reshape(samples, BS)
    left = jnp.concatenate([flat(rows, 1), flat(rows, 0)], axis=0)
    right = jnp.concatenate([flat(routed, 0), flat(routed, 1)], axis=0)
    left_hi, left_lo = split2(left)
    right_hi, right_lo = split2(right)
    dims = ((0,), (0,))
    total = dot(left_hi, right_hi, dims) + dot(left_hi, right_lo, dims) + dot(left_lo, right_hi, dims)
    stepped = tile[0] - (step_size * 0.5 / samples) * total
    i = lax.broadcasted_iota(jnp.int32, (BS, BS), 0)
    j = lax.broadcasted_iota(jnp.int32, (BS, BS), 1)
    flag = jnp.full((BS, BS), info[TD + t], jnp.int32)
    stepped = jnp.where((i == j) & (flag != 0), 0.0, stepped)
    limit = step_size * penalty
    out[0] = stepped - jnp.clip(stepped, -limit, limit)


def index_table(tile_rows, tile_cols, row, me):
    y, z = row // Z, row % Z
    groups = Y * Z
    tiles = C * TD
    wanted = ((y + jnp.arange(Y)) % Y) * Z + z
    take = wanted[:, None, None] == jnp.arange(groups)[None, :, None]
    cols = jnp.sum(jnp.where(take, tile_cols.reshape(1, groups, tiles), 0), axis=1)
    rows = jnp.sum(jnp.where(take[0], tile_rows.reshape(groups, tiles), 0), axis=0)
    source, local = cols // BLK, cols % BLK
    place = jnp.arange(tiles)
    rank = jnp.sum(
        (source[:, :, None] == source[:, None, :]) & (place[None, :] < place[:, None])[None],
        axis=2,
        dtype=jnp.int32,
    )
    slot = jnp.arange(SLOTS)
    chosen = (source[1:, None, :] == y * Z + slot[None, :, None] // CAP) & (
        rank[1:, None, :] == slot[None, :, None] % CAP
    )
    pick = jnp.sum(jnp.where(chosen, local[1:, None, :], 0), axis=2).reshape(-1)
    plane, depth = source[0] // Z, source[0] % Z
    away = (y - plane + Y) % Y
    fwd = jnp.where(
        away == 0,
        depth * BLK + local[0],
        PLANE + (away - 1) * SLOTS + depth * CAP + rank[0],
    )
    local_rows = rows - row * BLK
    before = (local_rows[None, :] < local_rows[:, None]) | (
        (local_rows[None, :] == local_rows[:, None]) & (place[None, :] < place[:, None])
    )
    position = jnp.sum(before, axis=1, dtype=jnp.int32)
    at = position[None, :] == place[:, None]
    lands = ((place // TD - me + C) % C) * TD + place % TD
    order = jnp.sum(jnp.where(at, lands[None, :], 0), axis=1)
    first = jnp.sum(local_rows[None, :] < local_rows[:, None], axis=1, dtype=jnp.int32)
    same = jnp.sum(jnp.where(at, (position > first)[None, :].astype(jnp.int32), 0), axis=1)
    blocks = jnp.arange(BLK)
    upto = jnp.sum(local_rows[None, :] <= blocks[:, None], axis=1, dtype=jnp.int32)
    count = jnp.sum(local_rows[None, :] == blocks[:, None], axis=1, dtype=jnp.int32)
    mine = (me * TD + jnp.arange(TD))[:, None] == place[None, :]
    my_rows = jnp.sum(jnp.where(mine, local_rows[None, :], 0), axis=1)
    on_diag = jnp.sum(jnp.where(mine, (rows == cols[0])[None, :].astype(jnp.int32), 0), axis=1)
    table = jnp.concatenate(
        [pick, fwd, order, same, jnp.maximum(upto - 1, 0), (count > 0).astype(jnp.int32), on_diag]
    )
    return table.astype(jnp.int32), jnp.concatenate([my_rows, on_diag]).astype(jnp.int32)


def per_device(samples, loadings, omega_tiles, omega_diagonal, tile_rows, tile_cols):
    row = lax.axis_index("rows")
    me = lax.axis_index("cols")
    factors = loadings.shape[0]
    ns = NC * SC
    table, info = index_table(tile_rows, tile_cols, row, me)
    f32 = jnp.float32
    vmem = lambda *shape: pltpu.VMEM(shape, f32)
    dma = lambda *shape: pltpu.SemaphoreType.DMA(shape)
    in_vmem = pl.BlockSpec(memory_space=pltpu.VMEM)
    anywhere = pl.BlockSpec(memory_space=pl.ANY)
    n = 2 * NC
    routed, group, new_diagonal = pl.pallas_call(
        route_kernel,
        out_shape=(
            jax.ShapeDtypeStruct((2, NC, C, TD, SC, BS), f32),
            jax.ShapeDtypeStruct((2, NC, C, BLK, SC, BS), f32),
            jax.ShapeDtypeStruct((BLK, BS), f32),
        ),
        in_specs=[
            pl.BlockSpec(memory_space=pltpu.SMEM),
            in_vmem,
            in_vmem,
            in_vmem,
            anywhere,
        ],
        out_specs=(anywhere, anywhere, in_vmem),
        scratch_shapes=[
            vmem(2, ns, factors),
            vmem(Z, ns, factors),
            vmem(Y, ns, factors),
            vmem(BLK, SC, BS),
            vmem(C * TD, SC, BS),
            vmem(TD, BS, BS),
            pltpu.VMEM((TD, BS, BS), jnp.bfloat16),
            pltpu.VMEM((TD, BS, BS), jnp.bfloat16),
            vmem(2, NC, C, BLK, SC, BS),
        ]
        + [vmem(PLANE + (Y - 1) * SLOTS, SC, BS)] * n
        + [vmem((Y - 1) * SLOTS, SC, BS)] * n
        + [vmem(C, TD, SC, BS)] * n
        + [vmem(C, TD, SC, BS)] * n
        + [vmem(C * TD, SC, BS)] * NC
        + [vmem(C * TD, SC, BS)] * NC
        + [
            dma(2),
            dma(2),
            dma(2, NC, 2),
            dma(2, NC, 2, Z // 2 + 1),
            dma(2, NC, Y - 1),
            dma(2, NC, Y - 1),
            dma(2, NC),
            dma(2, NC),
            dma(NC),
            dma(NC),
            dma(2, NC),
            dma(2, NC),
            dma(2 + n),
        ],
        compiler_params=pltpu.CompilerParams(
            collective_id=0, has_side_effects=True, vmem_limit_bytes=56 * 1024 * 1024
        ),
        name="route",
    )(table, samples, loadings, omega_diagonal.reshape(BLK, BS), omega_tiles)

    new_tiles = pl.pallas_call(
        step_kernel,
        out_shape=jax.ShapeDtypeStruct(omega_tiles.shape, f32),
        grid_spec=pltpu.PrefetchScalarGridSpec(
            num_scalar_prefetch=1,
            grid=(TD,),
            in_specs=[
                pl.BlockSpec((2, NC, C, None, SC, BS), lambda t, info: (0, 0, 0, t, 0, 0)),
                pl.BlockSpec((2, NC, C, None, SC, BS), lambda t, info: (0, 0, 0, info[t], 0, 0)),
                pl.BlockSpec((1, BS, BS), lambda t, info: (t, 0, 0)),
            ],
            out_specs=pl.BlockSpec((1, BS, BS), lambda t, info: (t, 0, 0)),
        ),
        compiler_params=pltpu.CompilerParams(vmem_limit_bytes=32 * 1024 * 1024),
        name="step",
    )(info, routed, group, omega_tiles)
    return new_tiles, new_diagonal.reshape(-1)


def solution(mesh):
    placed = (
        P("cols", "rows"),
        P(None, "rows"),
        P(("rows", "cols"), None, None),
        P("rows"),
        P(),
        P(),
    )
    return jax.shard_map(
        per_device,
        mesh=mesh,
        in_specs=placed,
        out_specs=(P(("rows", "cols"), None, None), P("rows")),
        check_vma=False,
    )
```

time: 479 us -> 148 us (0.31)
  waiting for transfers between devices: 156 us -> 0 us
  blocking collectives: 150 us -> 0 us
  Pallas kernels: 0 us -> 137 us
  starting transfers between devices: 79.4 us -> 0 us
  matrix products: 31.8 us -> 0 us
  local copies, waits for them, and re-layouts: 30.5 us -> 8.17 us
  other arithmetic: 15.9 us -> 1.57 us
  between operations: 14.7 us -> 0.79 us
    pallas_call x0 -> x2, Pallas kernels: none -> 137 us  [the longest x1 132 us: per_device(): pl.pallas_call(route_kernel, out_shape=(jax.ShapeDtypeStruct((2, NC, C, T...]
    all_to_all x4 -> x0, waiting for transfers between devices: 126 us -> none  [the longest x1 68.3 us: per_device(): lax.all_to_all(outbound(applied), 'rows', split_axis=1, concat_axis=1, ti...]
    unnamed x1 -> x0, blocking collectives: 119 us -> none
    all_to_all x4 -> x0, starting transfers between devices: 79.1 us -> none  [the longest x1 53.5 us: per_device(): lax.all_to_all(forward(arrived_resid), 'cols', split_axis=1, concat_axis=...]
    dot_general x6 -> x0, matrix products: 31.8 us -> none  [the longest x1 12 us: per_device(): jnp.einsum('ska,skb->kab', row_resid, routed_applied, precision=highest,...]
    all_gather x1 -> x0, blocking collectives: 30.8 us -> none  [per_device(): scores = lax.all_gather(shares, 'rows', axis=1, tiled=True)]
    reduce_scatter x1 -> x0, waiting for transfers between devices: 29.2 us -> none  [per_device(): lax.psum_scatter(partial_y, 'cols', scatter_dimension=0, tiled=True)]
    gather x6 -> x0, local copies, waits for them, and re-layouts: 15.5 us -> none  [the longest x2 5.04 us: forward(): jnp.take(flattened, forward_index, axis=1)]
  transfers between devices with their start and end apart: 7 -> 0, of which waited for: 4 -> 0; matrix products, arithmetic and copies ran while one was open for 7% -> 0% of each run, Pallas kernels for 0% -> 0%
where the time goes in v1:
time: 148 us
  Pallas kernels  137 us (93%)
  local copies, waits for them, and re-layouts  8.17 us (6%)
  other arithmetic  1.57 us (1%)
    pallas_call x1, Pallas kernels, per_device(): pl.pallas_call(route_kernel, out_shape=(jax.ShapeDtypeStruct((2, NC, C, T...  132 us
    pallas_call x1, Pallas kernels, per_device(): pl.pallas_call(step_kernel, out_shape=jax.ShapeDtypeStruct(omega_tiles.sh...  5.66 us
    unnamed x9, local copies, waits for them, and re-layouts  4.54 us

profile of v1, /device:TPU:1, one launch (start us, length us, event | category | flops | bytes accessed | tf_op | source)
XLA Modules:
  0.0 147.8 jit_solution(4685194790729293415)
XLA Ops:
  0.8 0.1 iota_compare_fusion.5
  0.9 1.3 reshape.214.diag
  2.2 0.8 reshape.212
  3.0 0.1 select_reduce_fusion.4
  3.1 0.2 fusion
  3.3 0.1 select_reduce_fusion.2
  3.4 0.1 convert_reduce_fusion.2
  3.5 0.8 broadcast_in_dim.127
  4.3 0.1 select_reduce_fusion
  4.4 0.2 select_reduce_fusion.6
  4.6 0.1 pad_add_fusion.info
  4.7 0.2 convert_reduce_fusion
  5.0 0.2 select_reduce_fusion.1
  5.2 0.1 reshape.213
  5.3 0.7 concatenate.7.meta
  6.0 0.0 copy-start
  6.0 131.6 %route.1 = (f32[2,2,8,5,8,512]{5,4,3,2,1,0:T(8,128)}, f32[2,2,8,8,8,512]{5,4,3,2,1,0:T(8,128)}, f32[8,512]{1,0:T(8,128)}) custom-call(s32[213]{0:T(256)} %concatenate.7.meta, f32[16,4096]{1,0:T(8,128)} %samples.1, bf16[256,4096]{1,0:T(8,128)(2,1)} %loadings.1, f32[8,512]{1,0:T(8,128)} %reshape.214.diag, f32[5,512,512]{2,1,0:T(8,128)} %tile.1), custom_call_target="tpu_custom_call" | custom-call | tf_op jit(solution)/shard_map/route/pallas_call | solution.py:469
  137.6 0.0 copy-done
  137.6 0.0 copy-start.1
  137.6 2.2 %copy-done.1 = f32[2,2,8,8,8,512]{5,4,3,2,1,0:T(8,128)S(1)} copy-done((f32[2,2,8,8,8,512]{5,4,3,2,1,0:T(8,128)S(1)}, f32[2,2,8,8,8,512]{5,4,3,2,1,0:T(8,128)}, u32[]{:S(2)}) %copy-start.1) | copy-done | bytes 4194328
  139.8 1.7 %copy-done.2 = f32[2,2,8,5,8,512]{5,4,3,2,1,0:T(8,128)S(1)} copy-done((f32[2,2,8,5,8,512]{5,4,3,2,1,0:T(8,128)S(1)}, f32[2,2,8,5,8,512]{5,4,3,2,1,0:T(8,128)}, u32[]{:S(2)}) %copy-start.2) | copy-done | bytes 2621464
  141.5 5.7 %step.1 = f32[5,512,512]{2,1,0:T(8,128)} custom-call(s32[10]{0:T(128)S(1)} %pad_add_fusion.info, f32[2,2,8,5,8,512]{5,4,3,2,1,0:T(8,128)S(1)} %copy-done.2, f32[2,2,8,8,8,512]{5,4,3,2,1,0:T(8,128)S(1)} %copy-done.1, f32[5,512,512]{2,1,0:T(8,128)S(1)} %copy-done), custom_call_target="tpu_custom_call" | custom-call | tf_op jit(solution)/shard_map/step/pallas_call | solution.py:522
  147.2 0.0 copy-done.3
  147.2 0.6 copy.8
  (18 shorter events, 0.2 us)
Async XLA Ops:
  6.0 131.6 %copy-start = (f32[5,512,512]{2,1,0:T(8,128)S(1)}, f32[5,512,512]{2,1,0:T(8,128)}, u32[]{:S(2)}) copy-start(f32[5,512,512]{2,1,0:T(8,128)} %tile.1) | copy-start | bytes 15728644
  137.6 2.2 %copy-start.1 = (f32[2,2,8,8,8,512]{5,4,3,2,1,0:T(8,128)S(1)}, f32[2,2,8,8,8,512]{5,4,3,2,1,0:T(8,128)}, u32[]{:S(2)}) copy-start(f32[2,2,8,8,8,512]{5,4,3,2,1,0:T(8,128)} %get-tuple-element.6.rows) | copy-start | bytes 12582916
  139.8 1.7 %copy-start.2 = (f32[2,2,8,5,8,512]{5,4,3,2,1,0:T(8,128)S(1)}, f32[2,2,8,5,8,512]{5,4,3,2,1,0:T(8,128)}, u32[]{:S(2)}) copy-start(f32[2,2,8,5,8,512]{5,4,3,2,1,0:T(8,128)} %get-tuple-element.5.routed) | copy-start | bytes 7864324
  141.5 5.7 %copy-start.3 = (f32[8,512]{1,0:T(8,128)S(1)}, f32[8,512]{1,0:T(8,128)}, u32[]{:S(2)}) copy-start(f32[8,512]{1,0:T(8,128)} %get-tuple-element.7) | copy-start | bytes 49156

commit v2 on v1

--- a/solution.py
+++ b/solution.py
@@ -63,6 +63,8 @@
     part,
     score_z,
     score_y,
+    score_c,
+    window,
     stage,
     seg,
     tile_f32,
@@ -89,6 +91,12 @@
         p_r,
         g_s,
         g_r,
+        h_s,
+        h_r,
+        w_s,
+        w_r,
+        v_s,
+        v_r,
         local,
     ) = rest[2 * NC :]
 
@@ -98,6 +106,8 @@
     at_z = lambda d: {"rows": y * Z + (z + d + Z) % Z}
     at_y = lambda d: {"rows": ((y + d) % Y) * Z + z}
     at_c = lambda d: {"cols": (me + d + C) % C}
+    side = 1 - 2 * (me % 2)
+    other = at_c(side)
 
     def remote(src, dst, send, recv, where):
         return pltpu.make_async_remote_copy(
@@ -129,6 +139,21 @@
     tile_copy = pltpu.make_async_copy(tiles, tile_f32, local.at[0])
     tile_copy.start()
 
+    def split_tiles(low, high):
+        rows = lax.broadcasted_iota(jnp.int32, (BS // 4, BS), 0)
+        cols = lax.broadcasted_iota(jnp.int32, (BS // 4, BS), 1)
+
+        def one(i):
+            t, q = i // 4, i % 4
+            at = pl.ds(pl.multiple_of(q * (BS // 4), BS // 4), BS // 4)
+            flag = jnp.full((BS // 4, BS), meta[DIAG + t], jnp.int32)
+            drop = (rows + q * (BS // 4) == cols) & (flag != 0)
+            hi, lo = split2(jnp.where(drop, 0.0, tile_f32[t, at]))
+            tile_hi[t, at] = hi
+            tile_lo[t, at] = lo
+
+        each(low, high, one)
+
     def score_step(b, total):
         cols = pl.ds(pl.multiple_of(b * BS, BS), BS)
         return total + dot(split3(samples[:, cols]), loadings[:, cols], ((1,), (1,)))
@@ -138,11 +163,40 @@
     part[0] = total[:ns] + total[ns : 2 * ns] + total[2 * ns :]
     pl.semaphore_wait(barrier, Z + Y + C - 3)
 
+    def gather_start(src, place, far_s, far_r, near_s, near_r):
+        each(
+            1,
+            C // 2,
+            lambda q: remote(src, place(2 * q), far_s.at[q], far_r.at[q], at_c(2 * q)).start(),
+        )
+        remote(src, place((side + C) % C), near_s.at[0], near_r.at[0], other).start()
+
+    def gather_pass(place, far_r, near_s, near_r):
+        def one(q):
+            wait_all(place(2 * q), far_r.at[q])
+            remote(
+                place(2 * q), place((side + 2 * q + C) % C), near_s.at[q], near_r.at[q], other
+            ).start()
+
+        each(1, C // 2, one)
+
+    def gathered(place, near_r):
+        each(0, C // 2, lambda q: wait_all(place((2 * q - side + C) % C), near_r.at[q]))
+
+    def gather_sent(place, far_s, near_s):
+        each(1, C // 2, lambda q: wait_all(place(2 * q), far_s.at[q]))
+        each(0, C // 2, lambda q: wait_all(place(2 * q), near_s.at[q]))
+
+    window_at = lambda d: window.at[d]
+
     each(
         1,
         Z,
         lambda d: remote(part.at[0], score_z.at[d], exch_s.at[0], exch_r.at[0], at_z(d)).start(),
     )
+    gather_start(samples, window_at, w_s, w_r, v_s, v_r)
+    tile_copy.wait()
+    split_tiles(0, 12)
     wait_all(score_z.at[pl.ds(1, Z - 1)], exch_r.at[0])
     total = part[0]
     for d in range(1, Z):
@@ -153,10 +207,12 @@
         Y,
         lambda d: remote(part.at[1], score_y.at[d], exch_s.at[1], exch_r.at[1], at_y(d)).start(),
     )
+    split_tiles(12, TD * 4)
     wait_all(score_y.at[pl.ds(1, Y - 1)], exch_r.at[1])
     for d in range(1, Y):
         total = total + score_y[d]
     scores = split3(total)
+    part[2] = total
 
     def residual_step(b):
         cols = pl.ds(pl.multiple_of(b * BS, BS), BS)
@@ -167,6 +223,22 @@
             group[0, h, 0, b] = value[h * SC : (h + 1) * SC]
 
     each(0, BLK, residual_step)
+
+    def group_residual():
+        gathered(window_at, v_r)
+        wait_all(score_c.at[pl.ds(1, C - 1)], exch_r.at[2])
+        far = (C - 1) * ns
+        terms3 = split3(score_c[1:].reshape(far, loadings.shape[0]))
+
+        def one(b):
+            cols = pl.ds(pl.multiple_of(b * BS, BS), BS)
+            terms = dot(terms3, loadings[:, cols], ((1,), (0,)))
+            terms = terms[:far] + terms[far : 2 * far] + terms[2 * far :]
+            value = window[pl.ds(1, C - 1), :, cols] - terms.reshape(C - 1, ns, BS)
+            for h in range(NC):
+                group[0, h, pl.ds(1, C - 1), b] = value[:, h * SC : (h + 1) * SC]
+
+        each(0, BLK, one)
 
     def hop(p, h, k, right):
         slice_of = ((z - k + 1 + Z) if right else (z + k - 1)) % Z
@@ -208,28 +280,25 @@
 
         each(0, Y - 1, to_plane)
 
-    def route(p, h, first=None, middle=None):
+    def ring_start(p, h):
         hop(p, h, 1, True).start()
         hop(p, h, 1, False).start()
-        send_picks(p, h, z)
-        if first:
-            first()
-
-        def step(k):
-            arrived(p, h, k, True)
-            hop(p, h, k + 1, True).start()
-            arrived(p, h, k, False)
-            hop(p, h, k + 1, False).start()
-            send_picks(p, h, (z - k + Z) % Z)
-            send_picks(p, h, (z + k) % Z)
-
-        each(1, Z // 2 - 1, step)
-        step(Z // 2 - 1)
-        if middle:
-            middle()
+
+    def ring_step(p, h, k):
+        arrived(p, h, k, True)
+        hop(p, h, k + 1, True).start()
+        arrived(p, h, k, False)
+        hop(p, h, k + 1, False).start()
+
+    def ring_end(p, h):
         arrived(p, h, Z // 2, True)
         arrived(p, h, Z // 2, False)
-        send_picks(p, h, (z + Z // 2) % Z)
+
+    def picks_at(p, h, k):
+        send_picks(p, h, (z - k + Z) % Z)
+        send_picks(p, h, (z + k) % Z)
+
+    def routed(p, h):
         for i in range(Y - 1):
             wait_all(field[p][h].at[pl.ds(PLANE + i * SLOTS, SLOTS)], y_r.at[p, h, i])
 
@@ -253,31 +322,6 @@
     def forwarded(p, h):
         wait_all(frecv[p][h].at[pl.ds(1, C - 1)], f_r.at[p, h])
 
-    def gather_start(p, h):
-        each(
-            1,
-            C,
-            lambda d: remote(
-                group.at[p, h, 0], group.at[p, h, d], g_s.at[p, h], g_r.at[p, h], at_c(d)
-            ).start(),
-        )
-
-    def split_tiles():
-        tile_copy.wait()
-        rows = lax.broadcasted_iota(jnp.int32, (BS // 4, BS), 0)
-        cols = lax.broadcasted_iota(jnp.int32, (BS // 4, BS), 1)
-
-        def one(i):
-            t, q = i // 4, i % 4
-            at = pl.ds(pl.multiple_of(q * (BS // 4), BS // 4), BS // 4)
-            flag = jnp.full((BS // 4, BS), meta[DIAG + t], jnp.int32)
-            drop = (rows + q * (BS // 4) == cols) & (flag != 0)
-            hi, lo = split2(jnp.where(drop, 0.0, tile_f32[t, at]))
-            tile_hi[t, at] = hi
-            tile_lo[t, at] = lo
-
-        each(0, TD * 4, one)
-
     def products(h):
         forwarded(0, h)
 
@@ -286,23 +330,22 @@
             both = dot(jnp.concatenate([hi, lo], axis=0), tile_hi[t], ((1,), (1,)))
             value = both[: C * SC] + both[C * SC :] + dot(hi, tile_lo[t], ((1,), (1,)))
             value = value.reshape(C, SC, BS)
-            for d in range(C):
+            precv[h][t] = value[0]
+            for d in range(1, C):
                 psend[h][d * TD + t] = value[d]
+            each(
+                1,
+                C,
+                lambda d: remote(
+                    psend[h].at[d * TD + t],
+                    precv[h].at[d * TD + t],
+                    p_s.at[h],
+                    p_r.at[h],
+                    at_c(-d),
+                ).start(),
+            )
 
         each(0, TD, one)
-        each(
-            1,
-            C,
-            lambda d: remote(
-                psend[h].at[pl.ds(d * TD, TD)],
-                precv[h].at[pl.ds(d * TD, TD)],
-                p_s.at[h],
-                p_r.at[h],
-                at_c(-d),
-            ).start(),
-        )
-        for t in range(TD):
-            precv[h][t] = psend[h][t]
 
     def apply_rows(h):
         wait_all(precv[h].at[pl.ds(TD, (C - 1) * TD)], p_r.at[h])
@@ -324,28 +367,82 @@
 
         each(0, BLK, block)
 
-    def start_gathers():
-        for h in range(NC):
-            gather_start(0, h)
-
-    route(0, 0, first=start_gathers, middle=split_tiles)
+    group_at = lambda h: lambda d: group.at[1, h, d]
+
+    def rows_start(h):
+        gather_start(group.at[1, h, 0], group_at(h), g_s.at[h], g_r.at[h], h_s.at[h], h_r.at[h])
+
+    def rows_pass(h):
+        gather_pass(group_at(h), g_r.at[h], h_s.at[h], h_r.at[h])
+
+    ring_start(0, 0)
+    send_picks(0, 0, z)
+    ring_start(0, 1)
+    send_picks(0, 1, z)
+    each(
+        1,
+        C,
+        lambda d: remote(part.at[2], score_c.at[d], exch_s.at[2], exch_r.at[2], at_c(d)).start(),
+    )
+
+    def both(k):
+        ring_step(0, 0, k)
+        picks_at(0, 0, k)
+        ring_step(0, 1, k)
+
+    each(1, Z // 2 - 1, both)
+    both(Z // 2 - 1)
+    gather_pass(window_at, w_r, v_s, v_r)
+    ring_end(0, 0)
+    send_picks(0, 0, (z + Z // 2) % Z)
+    each(1, Z // 2, lambda k: picks_at(0, 1, k))
+    ring_end(0, 1)
+    send_picks(0, 1, (z + Z // 2) % Z)
+    group_residual()
+    routed(0, 0)
     forward(0, 0)
-    route(0, 1, middle=lambda: products(0))
+    products(0)
+    routed(0, 1)
     forward(0, 1)
+
     apply_rows(0)
-    route(1, 0, first=lambda: gather_start(1, 0), middle=lambda: products(1))
+    ring_start(1, 0)
+    send_picks(1, 0, z)
+    rows_start(0)
+    ring_step(1, 0, 1)
+    picks_at(1, 0, 1)
+    ring_step(1, 0, 2)
+    picks_at(1, 0, 2)
+    products(1)
+    ring_step(1, 0, 3)
+    picks_at(1, 0, 3)
+    ring_end(1, 0)
+    send_picks(1, 0, (z + Z // 2) % Z)
+    rows_pass(0)
+    apply_rows(1)
+    ring_start(1, 1)
+    send_picks(1, 1, z)
+    rows_start(1)
+    ring_step(1, 1, 1)
+    picks_at(1, 1, 1)
+    ring_step(1, 1, 2)
+    picks_at(1, 1, 2)
+    routed(1, 0)
     forward(1, 0)
-    apply_rows(1)
-    route(1, 1, first=lambda: gather_start(1, 1))
+    ring_step(1, 1, 3)
+    picks_at(1, 1, 3)
+    ring_end(1, 1)
+    send_picks(1, 1, (z + Z // 2) % Z)
+    rows_pass(1)
+    for h in range(NC):
+        gathered(group_at(h), h_r.at[h])
+    routed(1, 1)
     forward(1, 1)
 
     def out_copy(src, dst):
         copy = pltpu.make_async_copy(src, dst, local.at[1])
         copy.start()
 
-    for p in range(2):
-        for h in range(NC):
-            wait_all(group.at[p, h, pl.ds(1, C - 1)], g_r.at[p, h])
     out_copy(group, group_out)
 
     def diag_step(b):
@@ -367,6 +464,8 @@
 
     wait_all(score_z.at[pl.ds(1, Z - 1)], exch_s.at[0])
     wait_all(score_y.at[pl.ds(1, Y - 1)], exch_s.at[1])
+    wait_all(score_c.at[pl.ds(1, C - 1)], exch_s.at[2])
+    gather_sent(window_at, w_s, v_s)
     sent = Z // 2 * BLK - BLK // 2
     for p in range(2):
         for h in range(NC):
@@ -375,9 +474,9 @@
             for i in range(Y - 1):
                 wait_all(ysend[p][h].at[pl.ds(i * SLOTS, SLOTS)], y_s.at[p, h, i])
             wait_all(fsend[p][h].at[pl.ds(1, C - 1)], f_s.at[p, h])
-            wait_all(group.at[p, h, pl.ds(1, C - 1)], g_s.at[p, h])
     for h in range(NC):
         wait_all(psend[h].at[pl.ds(TD, (C - 1) * TD)], p_s.at[h])
+        gather_sent(group_at(h), g_s.at[h], h_s.at[h])
     pltpu.make_async_copy(group, group_out, local.at[1]).wait()
     for p in range(2):
         for h in range(NC):
@@ -482,9 +581,11 @@
         ],
         out_specs=(anywhere, anywhere, in_vmem),
         scratch_shapes=[
-            vmem(2, ns, factors),
+            vmem(3, ns, factors),
             vmem(Z, ns, factors),
             vmem(Y, ns, factors),
+            vmem(C, ns, factors),
+            vmem(C, ns, BLK * BS),
             vmem(BLK, SC, BS),
             vmem(C * TD, SC, BS),
             vmem(TD, BS, BS),
@@ -499,8 +600,8 @@
         + [vmem(C * TD, SC, BS)] * NC
         + [vmem(C * TD, SC, BS)] * NC
         + [
-            dma(2),
-            dma(2),
+            dma(3),
+            dma(3),
             dma(2, NC, 2),
             dma(2, NC, 2, Z // 2 + 1),
             dma(2, NC, Y - 1),
@@ -509,8 +610,14 @@
             dma(2, NC),
             dma(NC),
             dma(NC),
-            dma(2, NC),
-            dma(2, NC),
+            dma(NC, C // 2),
+            dma(NC, C // 2),
+            dma(NC, C // 2),
+            dma(NC, C // 2),
+            dma(C // 2),
+            dma(C // 2),
+            dma(C // 2),
+            dma(C // 2),
             dma(2 + n),
         ],
         compiler_params=pltpu.CompilerParams(

time: 148 us -> 138 us (0.932)
  Pallas kernels: 137 us -> 127 us
    pallas_call x1, Pallas kernels: 132 us -> 121 us  [per_device(): pl.pallas_call(route_kernel, out_shape=(jax.ShapeDtypeStruct((2, NC, C, T...]
where the time goes in v2:
time: 138 us; the launch traced here: 137 us
  Pallas kernels  127 us (92%)
  local copies, waits for them, and re-layouts  8.17 us (6%)
  other arithmetic  1.57 us (1%)
    pallas_call x1, Pallas kernels, per_device(): pl.pallas_call(route_kernel, out_shape=(jax.ShapeDtypeStruct((2, NC, C, T...  121 us
    pallas_call x1, Pallas kernels, per_device(): pl.pallas_call(step_kernel, out_shape=jax.ShapeDtypeStruct(omega_tiles.sh...  5.65 us
    unnamed x9, local copies, waits for them, and re-layouts  4.54 us

profile of v2, /device:TPU:1, one launch (start us, length us, event | category | flops | bytes accessed | tf_op | source)
XLA Modules:
  0.0 137.3 jit_solution(1474146362369514672)
XLA Ops:
  0.8 0.1 iota_compare_fusion.5
  0.9 1.3 reshape.214.diag
  2.2 0.8 reshape.212
  3.0 0.1 select_reduce_fusion.4
  3.1 0.2 fusion
  3.3 0.1 select_reduce_fusion.2
  3.4 0.1 convert_reduce_fusion.2
  3.5 0.8 broadcast_in_dim.127
  4.3 0.1 select_reduce_fusion
  4.4 0.2 select_reduce_fusion.6
  4.6 0.1 pad_add_fusion.info
  4.7 0.2 convert_reduce_fusion
  5.0 0.2 select_reduce_fusion.1
  5.2 0.1 reshape.213
  5.3 0.7 concatenate.7.meta
  6.0 0.0 copy-start
  6.0 121.1 %route.1 = (f32[2,2,8,5,8,512]{5,4,3,2,1,0:T(8,128)}, f32[2,2,8,8,8,512]{5,4,3,2,1,0:T(8,128)}, f32[8,512]{1,0:T(8,128)}) custom-call(s32[213]{0:T(256)} %concatenate.7.meta, f32[16,4096]{1,0:T(8,128)} %samples.1, bf16[256,4096]{1,0:T(8,128)(2,1)} %loadings.1, f32[8,512]{1,0:T(8,128)} %reshape.214.diag, f32[5,512,512]{2,1,0:T(8,128)} %tile.1), custom_call_target="tpu_custom_call" | custom-call | tf_op jit(solution)/shard_map/route/pallas_call | solution.py:568
  127.1 0.0 copy-done
  127.1 0.0 copy-start.1
  127.1 2.2 %copy-done.1 = f32[2,2,8,8,8,512]{5,4,3,2,1,0:T(8,128)S(1)} copy-done((f32[2,2,8,8,8,512]{5,4,3,2,1,0:T(8,128)S(1)}, f32[2,2,8,8,8,512]{5,4,3,2,1,0:T(8,128)}, u32[]{:S(2)}) %copy-start.1) | copy-done | bytes 4194328
  129.3 1.7 %copy-done.2 = f32[2,2,8,5,8,512]{5,4,3,2,1,0:T(8,128)S(1)} copy-done((f32[2,2,8,5,8,512]{5,4,3,2,1,0:T(8,128)S(1)}, f32[2,2,8,5,8,512]{5,4,3,2,1,0:T(8,128)}, u32[]{:S(2)}) %copy-start.2) | copy-done | bytes 2621464
  131.0 5.7 %step.1 = f32[5,512,512]{2,1,0:T(8,128)} custom-call(s32[10]{0:T(128)S(1)} %pad_add_fusion.info, f32[2,2,8,5,8,512]{5,4,3,2,1,0:T(8,128)S(1)} %copy-done.2, f32[2,2,8,8,8,512]{5,4,3,2,1,0:T(8,128)S(1)} %copy-done.1, f32[5,512,512]{2,1,0:T(8,128)S(1)} %copy-done), custom_call_target="tpu_custom_call" | custom-call | tf_op jit(solution)/shard_map/step/pallas_call | solution.py:629
  136.6 0.0 copy-done.3
  136.6 0.6 copy.8
  (18 shorter events, 0.2 us)
Async XLA Ops:
  6.0 121.1 %copy-start = (f32[5,512,512]{2,1,0:T(8,128)S(1)}, f32[5,512,512]{2,1,0:T(8,128)}, u32[]{:S(2)}) copy-start(f32[5,512,512]{2,1,0:T(8,128)} %tile.1) | copy-start | bytes 15728644
  127.1 2.2 %copy-start.1 = (f32[2,2,8,8,8,512]{5,4,3,2,1,0:T(8,128)S(1)}, f32[2,2,8,8,8,512]{5,4,3,2,1,0:T(8,128)}, u32[]{:S(2)}) copy-start(f32[2,2,8,8,8,512]{5,4,3,2,1,0:T(8,128)} %get-tuple-element.6.rows) | copy-start | bytes 12582916
  129.2 1.7 %copy-start.2 = (f32[2,2,8,5,8,512]{5,4,3,2,1,0:T(8,128)S(1)}, f32[2,2,8,5,8,512]{5,4,3,2,1,0:T(8,128)}, u32[]{:S(2)}) copy-start(f32[2,2,8,5,8,512]{5,4,3,2,1,0:T(8,128)} %get-tuple-element.5.routed) | copy-start | bytes 7864324
  131.0 5.7 %copy-start.3 = (f32[8,512]{1,0:T(8,128)S(1)}, f32[8,512]{1,0:T(8,128)}, u32[]{:S(2)}) copy-start(f32[8,512]{1,0:T(8,128)} %get-tuple-element.7) | copy-start | bytes 49156

commit v3 on v2

--- a/solution.py
+++ b/solution.py
@@ -28,7 +28,8 @@
 LAST = SAME + C * TD
 HAS = LAST + BLK
 DIAG = HAS + BLK
-META = DIAG + TD
+ROWS = DIAG + TD
+META = ROWS + TD
 
 
 def split2(x):
@@ -57,8 +58,7 @@
     loadings,
     diag,
     tiles,
-    routed_out,
-    group_out,
+    tiles_out,
     diag_out,
     part,
     score_z,
@@ -70,13 +70,12 @@
     tile_f32,
     tile_hi,
     tile_lo,
-    group,
     *rest,
 ):
     n = 2 * NC
     pair = lambda flat: (flat[:NC], flat[NC:])
-    field, ysend, fsend, frecv = (pair(rest[i * n : (i + 1) * n]) for i in range(4))
-    rest = rest[4 * n :]
+    field, ysend, fsend, frecv, group = (pair(rest[i * n : (i + 1) * n]) for i in range(5))
+    rest = rest[5 * n :]
     psend, precv = rest[:NC], rest[NC : 2 * NC]
     (
         exch_s,
@@ -220,7 +219,7 @@
         value = samples[:, cols] - (terms[:ns] + terms[ns : 2 * ns] + terms[2 * ns :])
         for h in range(NC):
             field[0][h][z * BLK + b] = value[h * SC : (h + 1) * SC]
-            group[0, h, 0, b] = value[h * SC : (h + 1) * SC]
+            group[0][h][0, b] = value[h * SC : (h + 1) * SC]
 
     each(0, BLK, residual_step)
 
@@ -236,31 +235,28 @@
             terms = terms[:far] + terms[far : 2 * far] + terms[2 * far :]
             value = window[pl.ds(1, C - 1), :, cols] - terms.reshape(C - 1, ns, BS)
             for h in range(NC):
-                group[0, h, pl.ds(1, C - 1), b] = value[:, h * SC : (h + 1) * SC]
+                group[0][h][pl.ds(1, C - 1), b] = value[:, h * SC : (h + 1) * SC]
 
         each(0, BLK, one)
 
-    def hop(p, h, k, right):
+    half = BLK // 2
+
+    def hop(p, h, k, u, right):
         slice_of = ((z - k + 1 + Z) if right else (z + k - 1)) % Z
-        ref = field[p][h]
-        last = isinstance(k, int) and k == Z // 2
-        low = slice_of * BLK + (0 if right or not last else BLK // 2)
-        where = pl.ds(low, BLK // 2 if last else BLK)
+        ref = field[p][h].at[pl.ds(slice_of * BLK + u * half, half)]
         way = 0 if right else 1
         return remote(
-            ref.at[where],
-            ref.at[where],
+            ref,
+            ref,
             ring_s.at[p, h, way],
-            ring_r.at[p, h, way, k],
+            ring_r.at[p, h, way, k, u],
             at_z(1 if right else -1),
         )
 
-    def arrived(p, h, k, right):
+    def arrived(p, h, k, u, right):
         slice_of = ((z - k + Z) if right else (z + k)) % Z
-        last = isinstance(k, int) and k == Z // 2
-        low = slice_of * BLK + (0 if right or not last else BLK // 2)
-        ref = field[p][h].at[pl.ds(low, BLK // 2 if last else BLK)]
-        wait_all(ref, ring_r.at[p, h, 0 if right else 1, k])
+        ref = field[p][h].at[pl.ds(slice_of * BLK + u * half, half)]
+        wait_all(ref, ring_r.at[p, h, 0 if right else 1, k, u])
 
     def send_picks(p, h, zs):
         ref = field[p][h]
@@ -281,18 +277,24 @@
         each(0, Y - 1, to_plane)
 
     def ring_start(p, h):
-        hop(p, h, 1, True).start()
-        hop(p, h, 1, False).start()
-
-    def ring_step(p, h, k):
-        arrived(p, h, k, True)
-        hop(p, h, k + 1, True).start()
-        arrived(p, h, k, False)
-        hop(p, h, k + 1, False).start()
+        for u in range(2):
+            hop(p, h, 1, u, True).start()
+            hop(p, h, 1, 1 - u, False).start()
+
+    def ring_step(p, h, k, last=False):
+        for u in range(2):
+            arrived(p, h, k, u, True)
+            if not last or u == 0:
+                hop(p, h, k + 1, u, True).start()
+            arrived(p, h, k, 1 - u, False)
+            if not last or u == 0:
+                hop(p, h, k + 1, 1 - u, False).start()
+        picks_at(p, h, k)
 
     def ring_end(p, h):
-        arrived(p, h, Z // 2, True)
-        arrived(p, h, Z // 2, False)
+        arrived(p, h, Z // 2, 0, True)
+        arrived(p, h, Z // 2, 1, False)
+        send_picks(p, h, (z + Z // 2) % Z)
 
     def picks_at(p, h, k):
         send_picks(p, h, (z - k + Z) % Z)
@@ -303,30 +305,31 @@
             wait_all(field[p][h].at[pl.ds(PLANE + i * SLOTS, SLOTS)], y_r.at[p, h, i])
 
     def forward(p, h):
-        def one(d):
-            dest = (me + d) % C
-            for t in range(TD):
-                fsend[p][h][d, t] = field[p][h][meta[FWD + dest * TD + t]]
-            remote(
-                fsend[p][h].at[d],
-                frecv[p][h].at[d],
-                f_s.at[p, h],
-                f_r.at[p, h],
-                at_c(d),
-            ).start()
-
-        each(1, C, one)
-        for t in range(TD):
-            frecv[p][h][0, t] = field[p][h][meta[FWD + me * TD + t]]
-
-    def forwarded(p, h):
-        wait_all(frecv[p][h].at[pl.ds(1, C - 1)], f_r.at[p, h])
+        def tile(t):
+            def one(d):
+                dest = (me + d) % C
+                at = d * TD + t
+                fsend[p][h][at] = field[p][h][meta[FWD + dest * TD + t]]
+                remote(
+                    fsend[p][h].at[at],
+                    frecv[p][h].at[t, d],
+                    f_s.at[p, h],
+                    f_r.at[p, h, t],
+                    at_c(d),
+                ).start()
+
+            each(1, C, one)
+            frecv[p][h][t, 0] = field[p][h][meta[FWD + me * TD + t]]
+
+        each(0, TD, tile)
+
+    def forwarded(p, h, t):
+        wait_all(frecv[p][h].at[t, pl.ds(1, C - 1)], f_r.at[p, h, t])
 
     def products(h):
-        forwarded(0, h)
-
         def one(t):
-            hi, lo = split2(frecv[0][h][:, t].reshape(C * SC, BS))
+            forwarded(0, h, t)
+            hi, lo = split2(frecv[0][h][t].reshape(C * SC, BS))
             both = dot(jnp.concatenate([hi, lo], axis=0), tile_hi[t], ((1,), (1,)))
             value = both[: C * SC] + both[C * SC :] + dot(hi, tile_lo[t], ((1,), (1,)))
             value = value.reshape(C, SC, BS)
@@ -361,47 +364,78 @@
         def block(b):
             has = jnp.full((SC, BS), meta[HAS + b], jnp.int32) != 0
             value = jnp.where(has, seg[meta[LAST + b]], 0.0)
-            value = value + diag[pl.ds(b, 1)] * group[0, h, 0, b]
+            value = value + diag[pl.ds(b, 1)] * group[0][h][0, b]
             field[1][h][z * BLK + b] = value
-            group[1, h, 0, b] = value
+            group[1][h][0, b] = value
 
         each(0, BLK, block)
 
-    group_at = lambda h: lambda d: group.at[1, h, d]
+    group_at = lambda h: lambda d: group[1][h].at[d]
 
     def rows_start(h):
-        gather_start(group.at[1, h, 0], group_at(h), g_s.at[h], g_r.at[h], h_s.at[h], h_r.at[h])
+        gather_start(group[1][h].at[0], group_at(h), g_s.at[h], g_r.at[h], h_s.at[h], h_r.at[h])
 
     def rows_pass(h):
         gather_pass(group_at(h), g_r.at[h], h_s.at[h], h_r.at[h])
 
+    scale = step_size * 0.5 / (NC * C * SC)
+
+    def gradient_step(h, finish):
+        def one(t):
+            forwarded(1, h, t)
+            block = meta[ROWS + t]
+            rows = lambda p: group[p][h][:, block].reshape(C * SC, BS)
+            left_hi, left_lo = split2(jnp.concatenate([rows(1), rows(0)], axis=0))
+            right = [frecv[p][h][t].reshape(C * SC, BS) for p in range(2)]
+            right_hi, right_lo = split2(jnp.concatenate(right, axis=0))
+            left = jnp.concatenate([left_hi, left_hi, left_lo], axis=0)
+            right = jnp.concatenate([right_hi, right_lo, right_hi], axis=0)
+            total = dot(left, right, ((0,), (0,)))
+            stepped = tile_f32[t] - scale * total
+            if finish:
+                i = lax.broadcasted_iota(jnp.int32, (BS, BS), 0)
+                j = lax.broadcasted_iota(jnp.int32, (BS, BS), 1)
+                flag = jnp.full((BS, BS), meta[DIAG + t], jnp.int32)
+                stepped = jnp.where((i == j) & (flag != 0), 0.0, stepped)
+                limit = step_size * penalty
+                stepped = stepped - jnp.clip(stepped, -limit, limit)
+            tile_f32[t] = stepped
+            if finish:
+                pltpu.make_async_copy(tile_f32.at[t], tiles_out.at[t], local.at[1 + t]).start()
+
+        each(0, TD, one)
+
+    def diag_step(b):
+        total = jnp.zeros((SC, BS), jnp.float32)
+        for h in range(NC):
+            for d in range(C):
+                total = total + group[0][h][d, b] * group[1][h][d, b]
+        stat = jnp.sum(total, axis=0, keepdims=True) / (NC * C * SC)
+        old = diag[pl.ds(b, 1)]
+        diag_out[pl.ds(b, 1)] = old - step_size * (stat - 1.0 / old)
+
+    far_step = Z // 2 - 1
+
     ring_start(0, 0)
     send_picks(0, 0, z)
-    ring_start(0, 1)
     send_picks(0, 1, z)
     each(
         1,
         C,
         lambda d: remote(part.at[2], score_c.at[d], exch_s.at[2], exch_r.at[2], at_c(d)).start(),
     )
-
-    def both(k):
-        ring_step(0, 0, k)
-        picks_at(0, 0, k)
-        ring_step(0, 1, k)
-
-    each(1, Z // 2 - 1, both)
-    both(Z // 2 - 1)
+    each(1, far_step, lambda k: ring_step(0, 0, k))
+    ring_step(0, 0, far_step, last=True)
+    ring_start(0, 1)
     gather_pass(window_at, w_r, v_s, v_r)
     ring_end(0, 0)
-    send_picks(0, 0, (z + Z // 2) % Z)
-    each(1, Z // 2, lambda k: picks_at(0, 1, k))
-    ring_end(0, 1)
-    send_picks(0, 1, (z + Z // 2) % Z)
-    group_residual()
+    each(1, far_step, lambda k: ring_step(0, 1, k))
     routed(0, 0)
     forward(0, 0)
+    ring_step(0, 1, far_step, last=True)
+    ring_end(0, 1)
     products(0)
+    group_residual()
     routed(0, 1)
     forward(0, 1)
 
@@ -409,58 +443,29 @@
     ring_start(1, 0)
     send_picks(1, 0, z)
     rows_start(0)
-    ring_step(1, 0, 1)
-    picks_at(1, 0, 1)
-    ring_step(1, 0, 2)
-    picks_at(1, 0, 2)
+    each(1, far_step, lambda k: ring_step(1, 0, k))
+    ring_step(1, 0, far_step, last=True)
     products(1)
-    ring_step(1, 0, 3)
-    picks_at(1, 0, 3)
     ring_end(1, 0)
-    send_picks(1, 0, (z + Z // 2) % Z)
     rows_pass(0)
+
     apply_rows(1)
     ring_start(1, 1)
     send_picks(1, 1, z)
-    rows_start(1)
-    ring_step(1, 1, 1)
-    picks_at(1, 1, 1)
-    ring_step(1, 1, 2)
-    picks_at(1, 1, 2)
     routed(1, 0)
     forward(1, 0)
-    ring_step(1, 1, 3)
-    picks_at(1, 1, 3)
+    rows_start(1)
+    each(1, far_step, lambda k: ring_step(1, 1, k))
+    ring_step(1, 1, far_step, last=True)
     ring_end(1, 1)
-    send_picks(1, 1, (z + Z // 2) % Z)
     rows_pass(1)
-    for h in range(NC):
-        gathered(group_at(h), h_r.at[h])
+    gathered(group_at(0), h_r.at[0])
+    gradient_step(0, False)
+    gathered(group_at(1), h_r.at[1])
+    each(0, BLK, diag_step)
     routed(1, 1)
     forward(1, 1)
-
-    def out_copy(src, dst):
-        copy = pltpu.make_async_copy(src, dst, local.at[1])
-        copy.start()
-
-    out_copy(group, group_out)
-
-    def diag_step(b):
-        total = jnp.zeros((SC, BS), jnp.float32)
-        for h in range(NC):
-            for d in range(C):
-                total = total + group[0, h, d, b] * group[1, h, d, b]
-        stat = jnp.sum(total, axis=0, keepdims=True) / (NC * C * SC)
-        old = diag[pl.ds(b, 1)]
-        diag_out[pl.ds(b, 1)] = old - step_size * (stat - 1.0 / old)
-
-    each(0, BLK, diag_step)
-    for p in range(2):
-        for h in range(NC):
-            if p == 1:
-                forwarded(p, h)
-            copy = pltpu.make_async_copy(frecv[p][h], routed_out.at[p, h], local.at[2 + p * NC + h])
-            copy.start()
+    gradient_step(1, True)
 
     wait_all(score_z.at[pl.ds(1, Z - 1)], exch_s.at[0])
     wait_all(score_y.at[pl.ds(1, Y - 1)], exch_s.at[1])
@@ -473,35 +478,12 @@
                 wait_all(field[p][h].at[pl.ds(0, sent)], ring_s.at[p, h, way])
             for i in range(Y - 1):
                 wait_all(ysend[p][h].at[pl.ds(i * SLOTS, SLOTS)], y_s.at[p, h, i])
-            wait_all(fsend[p][h].at[pl.ds(1, C - 1)], f_s.at[p, h])
+            wait_all(fsend[p][h].at[pl.ds(TD, (C - 1) * TD)], f_s.at[p, h])
     for h in range(NC):
         wait_all(psend[h].at[pl.ds(TD, (C - 1) * TD)], p_s.at[h])
         gather_sent(group_at(h), g_s.at[h], h_s.at[h])
-    pltpu.make_async_copy(group, group_out, local.at[1]).wait()
-    for p in range(2):
-        for h in range(NC):
-            pltpu.make_async_copy(
-                frecv[p][h], routed_out.at[p, h], local.at[2 + p * NC + h]
-            ).wait()
-
-
-def step_kernel(info, routed, rows, tile, out):
-    t = pl.program_id(0)
-    samples = NC * C * SC
-    flat = lambda ref, p: ref[p].reshape(samples, BS)
-    left = jnp.concatenate([flat(rows, 1), flat(rows, 0)], axis=0)
-    right = jnp.concatenate([flat(routed, 0), flat(routed, 1)], axis=0)
-    left_hi, left_lo = split2(left)
-    right_hi, right_lo = split2(right)
-    dims = ((0,), (0,))
-    total = dot(left_hi, right_hi, dims) + dot(left_hi, right_lo, dims) + dot(left_lo, right_hi, dims)
-    stepped = tile[0] - (step_size * 0.5 / samples) * total
-    i = lax.broadcasted_iota(jnp.int32, (BS, BS), 0)
-    j = lax.broadcasted_iota(jnp.int32, (BS, BS), 1)
-    flag = jnp.full((BS, BS), info[TD + t], jnp.int32)
-    stepped = jnp.where((i == j) & (flag != 0), 0.0, stepped)
-    limit = step_size * penalty
-    out[0] = stepped - jnp.clip(stepped, -limit, limit)
+    for t in range(TD):
+        pltpu.make_async_copy(tile_f32.at[t], tiles_out.at[t], local.at[1 + t]).wait()
 
 
 def index_table(tile_rows, tile_cols, row, me):
@@ -548,9 +530,9 @@
     my_rows = jnp.sum(jnp.where(mine, local_rows[None, :], 0), axis=1)
     on_diag = jnp.sum(jnp.where(mine, (rows == cols[0])[None, :].astype(jnp.int32), 0), axis=1)
     table = jnp.concatenate(
-        [pick, fwd, order, same, jnp.maximum(upto - 1, 0), (count > 0).astype(jnp.int32), on_diag]
-    )
-    return table.astype(jnp.int32), jnp.concatenate([my_rows, on_diag]).astype(jnp.int32)
+        [pick, fwd, order, same, jnp.maximum(upto - 1, 0), (count > 0).astype(jnp.int32), on_diag, my_rows]
+    )
+    return table.astype(jnp.int32)
 
 
 def per_device(samples, loadings, omega_tiles, omega_diagonal, tile_rows, tile_cols):
@@ -558,18 +540,17 @@
     me = lax.axis_index("cols")
     factors = loadings.shape[0]
     ns = NC * SC
-    table, info = index_table(tile_rows, tile_cols, row, me)
+    table = index_table(tile_rows, tile_cols, row, me)
     f32 = jnp.float32
     vmem = lambda *shape: pltpu.VMEM(shape, f32)
     dma = lambda *shape: pltpu.SemaphoreType.DMA(shape)
     in_vmem = pl.BlockSpec(memory_space=pltpu.VMEM)
     anywhere = pl.BlockSpec(memory_space=pl.ANY)
     n = 2 * NC
-    routed, group, new_diagonal = pl.pallas_call(
+    new_tiles, new_diagonal = pl.pallas_call(
         route_kernel,
         out_shape=(
-            jax.ShapeDtypeStruct((2, NC, C, TD, SC, BS), f32),
-            jax.ShapeDtypeStruct((2, NC, C, BLK, SC, BS), f32),
+            jax.ShapeDtypeStruct(omega_tiles.shape, f32),
             jax.ShapeDtypeStruct((BLK, BS), f32),
         ),
         in_specs=[
@@ -579,7 +560,7 @@
             in_vmem,
             anywhere,
         ],
-        out_specs=(anywhere, anywhere, in_vmem),
+        out_specs=(anywhere, in_vmem),
         scratch_shapes=[
             vmem(3, ns, factors),
             vmem(Z, ns, factors),
@@ -591,23 +572,23 @@
             vmem(TD, BS, BS),
             pltpu.VMEM((TD, BS, BS), jnp.bfloat16),
             pltpu.VMEM((TD, BS, BS), jnp.bfloat16),
-            vmem(2, NC, C, BLK, SC, BS),
         ]
         + [vmem(PLANE + (Y - 1) * SLOTS, SC, BS)] * n
         + [vmem((Y - 1) * SLOTS, SC, BS)] * n
-        + [vmem(C, TD, SC, BS)] * n
-        + [vmem(C, TD, SC, BS)] * n
+        + [vmem(C * TD, SC, BS)] * n
+        + [vmem(TD, C, SC, BS)] * n
+        + [vmem(C, BLK, SC, BS)] * n
         + [vmem(C * TD, SC, BS)] * NC
         + [vmem(C * TD, SC, BS)] * NC
         + [
             dma(3),
             dma(3),
             dma(2, NC, 2),
-            dma(2, NC, 2, Z // 2 + 1),
+            dma(2, NC, 2, Z // 2 + 1, 2),
             dma(2, NC, Y - 1),
             dma(2, NC, Y - 1),
             dma(2, NC),
-            dma(2, NC),
+            dma(2, NC, TD),
             dma(NC),
             dma(NC),
             dma(NC, C // 2),
@@ -618,7 +599,7 @@
             dma(C // 2),
             dma(C // 2),
             dma(C // 2),
-            dma(2 + n),
+            dma(1 + TD),
         ],
         compiler_params=pltpu.CompilerParams(
             collective_id=0, has_side_effects=True, vmem_limit_bytes=56 * 1024 * 1024
@@ -626,22 +607,6 @@
         name="route",
     )(table, samples, loadings, omega_diagonal.reshape(BLK, BS), omega_tiles)
 
-    new_tiles = pl.pallas_call(
-        step_kernel,
-        out_shape=jax.ShapeDtypeStruct(omega_tiles.shape, f32),
-        grid_spec=pltpu.PrefetchScalarGridSpec(
-            num_scalar_prefetch=1,
-            grid=(TD,),
-            in_specs=[
-                pl.BlockSpec((2, NC, C, None, SC, BS), lambda t, info: (0, 0, 0, t, 0, 0)),
-                pl.BlockSpec((2, NC, C, None, SC, BS), lambda t, info: (0, 0, 0, info[t], 0, 0)),
-                pl.BlockSpec((1, BS, BS), lambda t, info: (t, 0, 0)),
-            ],
-            out_specs=pl.BlockSpec((1, BS, BS), lambda t, info: (t, 0, 0)),
-        ),
-        compiler_params=pltpu.CompilerParams(vmem_limit_bytes=32 * 1024 * 1024),
-        name="step",
-    )(info, routed, group, omega_tiles)
     return new_tiles, new_diagonal.reshape(-1)
 
 

time: 138 us -> 131 us (0.949)
  Pallas kernels: 127 us -> 117 us
  local copies, waits for them, and re-layouts: 8.17 us -> 10.8 us
    pallas_call x2 -> x1, Pallas kernels: 127 us -> 117 us  [per_device(): pl.pallas_call(route_kernel, out_shape=(jax.ShapeDtypeStruct(omega_tiles....]
    unnamed x9 -> x2, local copies, waits for them, and re-layouts: 4.54 us -> 7.13 us
where the time goes in v3:
time: 131 us; the launch traced here: 130 us
  Pallas kernels  117 us (89%)
  local copies, waits for them, and re-layouts  10.8 us (8%)
  other arithmetic  1.49 us (1%)
    pallas_call x1, Pallas kernels, per_device(): pl.pallas_call(route_kernel, out_shape=(jax.ShapeDtypeStruct(omega_tiles....  117 us
    unnamed x2, local copies, waits for them, and re-layouts  7.13 us

profile of v3, /device:TPU:1, one launch (start us, length us, event | category | flops | bytes accessed | tf_op | source)
XLA Modules:
  0.0 130.3 jit_solution(1939085099638017529)
XLA Ops:
  0.8 0.1 iota_compare_fusion.5
  0.9 1.3 %reshape.215.diag = f32[8,512]{1,0:T(8,128)} reshape(f32[4096]{0:T(1024)} %param.9) | data formatting | bytes 32768 | tf_op jit(solution)/shard_map/reshape | solution.py:608
  2.2 0.8 reshape.214
  3.0 0.1 select_reduce_fusion.4
  3.1 0.1 convert_reduce_fusion.2
  3.2 0.2 fusion
  3.4 0.1 select_reduce_fusion.2
  3.5 0.8 broadcast_in_dim.122
  4.3 0.1 select_reduce_fusion
  4.4 0.2 select_reduce_fusion.5
  4.6 0.2 convert_reduce_fusion
  4.9 0.2 select_reduce_fusion.1
  5.1 0.1 reshape.213
  5.2 0.7 concatenate.3.meta
  5.9 117.3 %route.1 = (f32[5,512,512]{2,1,0:T(8,128)}, f32[8,512]{1,0:T(8,128)}) custom-call(s32[218]{0:T(256)} %concatenate.3.meta, f32[16,4096]{1,0:T(8,128)} %samples.1, bf16[256,4096]{1,0:T(8,128)(2,1)} %loadings.1, f32[8,512]{1,0:T(8,128)} %reshape.215.diag, f32[5,512,512]{2,1,0:T(8,128)} %tiles.1), custom_call_target="tpu_custom_call" | custom-call | tf_op jit(solution)/shard_map/route/pallas_call | solution.py:550
  123.1 1.3 %copy.8 = f32[1,4,8,128]{3,1,2,0:T(4,128)} copy(f32[1,4,8,128]{3,2,1,0:T(8,128)} %bitcast.31) | data formatting | bytes 32768
  124.5 5.8 %copy.10 = f32[5,512,512]{2,1,0:T(8,128)} copy(f32[5,512,512]{2,1,0:T(8,128)} %get-tuple-element.20) | data formatting | bytes 10485760
  (16 shorter events, 0.2 us)

commit v4 on v3

--- a/solution.py
+++ b/solution.py
@@ -364,7 +364,7 @@
         def block(b):
             has = jnp.full((SC, BS), meta[HAS + b], jnp.int32) != 0
             value = jnp.where(has, seg[meta[LAST + b]], 0.0)
-            value = value + diag[pl.ds(b, 1)] * group[0][h][0, b]
+            value = value + diag[:, pl.ds(pl.multiple_of(b * BS, BS), BS)] * group[0][h][0, b]
             field[1][h][z * BLK + b] = value
             group[1][h][0, b] = value
 
@@ -397,8 +397,6 @@
                 j = lax.broadcasted_iota(jnp.int32, (BS, BS), 1)
                 flag = jnp.full((BS, BS), meta[DIAG + t], jnp.int32)
                 stepped = jnp.where((i == j) & (flag != 0), 0.0, stepped)
-                limit = step_size * penalty
-                stepped = stepped - jnp.clip(stepped, -limit, limit)
             tile_f32[t] = stepped
             if finish:
                 pltpu.make_async_copy(tile_f32.at[t], tiles_out.at[t], local.at[1 + t]).start()
@@ -411,8 +409,9 @@
             for d in range(C):
                 total = total + group[0][h][d, b] * group[1][h][d, b]
         stat = jnp.sum(total, axis=0, keepdims=True) / (NC * C * SC)
-        old = diag[pl.ds(b, 1)]
-        diag_out[pl.ds(b, 1)] = old - step_size * (stat - 1.0 / old)
+        at = pl.ds(pl.multiple_of(b * BS, BS), BS)
+        old = diag[:, at]
+        diag_out[:, at] = old - step_size * (stat - 1.0 / old)
 
     far_step = Z // 2 - 1
 
@@ -436,12 +435,12 @@
     ring_end(0, 1)
     products(0)
     group_residual()
-    routed(0, 1)
-    forward(0, 1)
 
     apply_rows(0)
     ring_start(1, 0)
     send_picks(1, 0, z)
+    routed(0, 1)
+    forward(0, 1)
     rows_start(0)
     each(1, far_step, lambda k: ring_step(1, 0, k))
     ring_step(1, 0, far_step, last=True)
@@ -488,12 +487,10 @@
 
 def index_table(tile_rows, tile_cols, row, me):
     y, z = row // Z, row % Z
-    groups = Y * Z
     tiles = C * TD
-    wanted = ((y + jnp.arange(Y)) % Y) * Z + z
-    take = wanted[:, None, None] == jnp.arange(groups)[None, :, None]
-    cols = jnp.sum(jnp.where(take, tile_cols.reshape(1, groups, tiles), 0), axis=1)
-    rows = jnp.sum(jnp.where(take[0], tile_rows.reshape(groups, tiles), 0), axis=0)
+    of_group = lambda ids, g: lax.dynamic_slice(ids, (g * tiles,), (tiles,))
+    cols = jnp.stack([of_group(tile_cols, ((y + d) % Y) * Z + z) for d in range(Y)])
+    rows = of_group(tile_rows, row)
     source, local = cols // BLK, cols % BLK
     place = jnp.arange(tiles)
     rank = jnp.sum(
@@ -551,7 +548,7 @@
         route_kernel,
         out_shape=(
             jax.ShapeDtypeStruct(omega_tiles.shape, f32),
-            jax.ShapeDtypeStruct((BLK, BS), f32),
+            jax.ShapeDtypeStruct((1, BLK * BS), f32),
         ),
         in_specs=[
             pl.BlockSpec(memory_space=pltpu.SMEM),
@@ -602,11 +599,13 @@
             dma(1 + TD),
         ],
         compiler_params=pltpu.CompilerParams(
-            collective_id=0, has_side_effects=True, vmem_limit_bytes=56 * 1024 * 1024
+            collective_id=0, has_side_effects=True, vmem_limit_bytes=46 * 1024 * 1024
         ),
         name="route",
-    )(table, samples, loadings, omega_diagonal.reshape(BLK, BS), omega_tiles)
-
+    )(table, samples, loadings, omega_diagonal.reshape(1, BLK * BS), omega_tiles)
+
+    limit = step_size * penalty
+    new_tiles = new_tiles - jnp.clip(new_tiles, -limit, limit)
     return new_tiles, new_diagonal.reshape(-1)
 
 

time: 131 us -> 127 us (0.969)
  local copies, waits for them, and re-layouts: 10.8 us -> 4.98 us
  other arithmetic: 1.49 us -> 5.75 us
  Pallas kernels: 117 us -> 114 us
    unnamed x2 -> x7, local copies, waits for them, and re-layouts: 7.13 us -> 3.87 us
    sub x0 -> x1, other arithmetic: none -> 3.02 us  [per_device(): new_tiles = new_tiles - jnp.clip(new_tiles, -limit, limit)]
    pallas_call x1, Pallas kernels: 117 us -> 114 us  [per_device(): pl.pallas_call(route_kernel, out_shape=(jax.ShapeDtypeStruct(omega_tiles....]
    reshape x2 -> x0, local copies, waits for them, and re-layouts: 2.1 us -> none  [the longest x1 1.33 us: per_device(): omega_diagonal.reshape(BLK, BS)]
where the time goes in v4:
time: 127 us; the launch traced here: 126 us
  Pallas kernels  114 us (90%)
  other arithmetic  5.75 us (5%)
  local copies, waits for them, and re-layouts  4.98 us (4%)
    pallas_call x1, Pallas kernels, per_device(): pl.pallas_call(route_kernel, out_shape=(jax.ShapeDtypeStruct(omega_tiles....  114 us
    unnamed x7, local copies, waits for them, and re-layouts  3.87 us
    sub x1, other arithmetic, per_device(): new_tiles = new_tiles - jnp.clip(new_tiles, -limit, limit)  3.02 us

profile of v4, /device:TPU:1, one launch (start us, length us, event | category | flops | bytes accessed | tf_op | source)
XLA Modules:
  0.0 126.1 jit_solution(13727675614973893446)
XLA Ops:
  0.7 0.8 broadcast_subtract_fusion
  1.5 0.8 compare_convert_fusion.1
  2.4 0.9 dynamic-slice_bitcast_fusion.3
  3.3 0.2 select_reduce_fusion.3
  3.5 0.1 convert_reduce_fusion.2
  3.7 0.2 fusion
  3.8 0.1 select_reduce_fusion.1
  4.0 0.2 convert_reduce_fusion
  4.3 0.2 select_reduce_fusion
  4.5 0.1 reshape.351
  4.6 0.1 concatenate.29.meta
  4.7 0.0 copy-start
  4.7 1.6 %copy-done = bf16[256,4096]{1,0:T(8,128)(2,1)S(1)} copy-done((bf16[256,4096]{1,0:T(8,128)(2,1)S(1)}, bf16[256,4096]{1,0:T(8,128)(2,1)}, u32[]{:S(2)}) %copy-start) | copy-done | bytes 2097176
  6.3 0.0 copy-start.1
  6.3 0.9 copy-done.1
  7.2 0.0 copy-start.2
  7.2 0.7 copy-done.2
  7.9 114.5 %route.1 = (f32[5,512,512]{2,1,0:T(8,128)S(1)}, f32[1,4096]{1,0:T(1,128)S(1)}) custom-call(s32[218]{0:T(256)S(1)} %concatenate.29.meta, f32[16,4096]{1,0:T(8,128)S(1)} %copy-done.1, bf16[256,4096]{1,0:T(8,128)(2,1)S(1)} %copy-done, f32[1,4096]{1,0:T(1,128)S(1)} %bitcast.31, f32[5,512,512]{2,1,0:T(8,128)} %tiles.1), custom_call_target="tpu_custom_call" | custom-call | tf_op jit(solution)/shard_map/route/pallas_call | solution.py:547
  122.4 3.0 %clamp_subtract_fusion = f32[5,512,512]{2,1,0:T(8,128)} fusion(f32[5,512,512]{2,1,0:T(8,128)S(1)} %get-tuple-element.4), kind=kLoop, calls=%fused_computation | loop fusion | flops 2621440 | bytes 10485760 | tf_op jit(solution)/shard_map/sub | solution.py:608
  125.5 0.6 copy.9
  (12 shorter events, 0.1 us)
Async XLA Ops:
  4.7 1.6 %copy-start = (bf16[256,4096]{1,0:T(8,128)(2,1)S(1)}, bf16[256,4096]{1,0:T(8,128)(2,1)}, u32[]{:S(2)}) copy-start(bf16[256,4096]{1,0:T(8,128)(2,1)} %loadings.1) | copy-start | bytes 6291460
  6.3 0.9 copy-start.1
  7.2 0.7 copy-start.2

commit v5 on v4

--- a/solution.py
+++ b/solution.py
@@ -54,9 +54,9 @@
 
 def route_kernel(
     meta,
-    samples,
-    loadings,
-    diag,
+    samples_in,
+    loadings_in,
+    diag_in,
     tiles,
     tiles_out,
     diag_out,
@@ -67,6 +67,9 @@
     window,
     stage,
     seg,
+    samples,
+    loadings,
+    diag,
     tile_f32,
     tile_hi,
     tile_lo,
@@ -76,6 +79,8 @@
     pair = lambda flat: (flat[:NC], flat[NC:])
     field, ysend, fsend, frecv, group = (pair(rest[i * n : (i + 1) * n]) for i in range(5))
     rest = rest[5 * n :]
+    slots = (((rest[0], rest[1]), (rest[2],)), ((rest[3],), (rest[4], rest[5])))
+    rest = rest[6:]
     psend, precv = rest[:NC], rest[NC : 2 * NC]
     (
         exch_s,
@@ -135,6 +140,14 @@
     greet(at_z, Z)
     greet(at_y, Y)
     greet(at_c, C)
+    loads = [
+        pltpu.make_async_copy(src, dst, local.at[1 + TD + i])
+        for i, (src, dst) in enumerate(
+            ((samples_in, samples), (loadings_in, loadings), (diag_in, diag))
+        )
+    ]
+    for load in loads:
+        load.start()
     tile_copy = pltpu.make_async_copy(tiles, tile_f32, local.at[0])
     tile_copy.start()
 
@@ -157,6 +170,8 @@
         cols = pl.ds(pl.multiple_of(b * BS, BS), BS)
         return total + dot(split3(samples[:, cols]), loadings[:, cols], ((1,), (1,)))
 
+    for load in loads:
+        load.wait()
     ns = NC * SC
     total = lax.fori_loop(0, BLK, score_step, jnp.zeros((3 * ns, loadings.shape[0]), jnp.float32))
     part[0] = total[:ns] + total[ns : 2 * ns] + total[2 * ns :]
@@ -258,30 +273,39 @@
         ref = field[p][h].at[pl.ds(slice_of * BLK + u * half, half)]
         wait_all(ref, ring_r.at[p, h, 0 if right else 1, k, u])
 
-    def send_picks(p, h, zs):
-        ref = field[p][h]
-        stage[...] = ref[pl.ds(zs * BLK, BLK)]
+    def part_of(q):
+        return pl.ds(0, BS) if q is None else pl.ds(q * (BS // 2), BS // 2)
+
+    def send_slots(p, h, zs, i, q):
+        base = i * SLOTS + zs * CAP
+        remote(
+            ysend[p][h].at[pl.ds(base, CAP), :, part_of(q)],
+            slots[p][h][q or 0].at[pl.ds(base, CAP)],
+            y_s.at[p, h, i],
+            y_r.at[p, h, i, q or 0],
+            at_y(i + 1),
+        ).start()
+
+    def send_picks(p, h, zs, q=None):
+        stage[...] = field[p][h][pl.ds(zs * BLK, BLK)]
 
         def to_plane(i):
             base = i * SLOTS + zs * CAP
             for j in range(CAP):
                 ysend[p][h][base + j] = stage[meta[PICK + base + j]]
-            remote(
-                ysend[p][h].at[pl.ds(base, CAP)],
-                ref.at[pl.ds(PLANE + base, CAP)],
-                y_s.at[p, h, i],
-                y_r.at[p, h, i],
-                at_y(i + 1),
-            ).start()
+            send_slots(p, h, zs, i, q)
 
         each(0, Y - 1, to_plane)
+
+    def send_rest(p, h):
+        each(0, Z * (Y - 1), lambda a: send_slots(p, h, (z + a // (Y - 1)) % Z, a % (Y - 1), 1))
 
     def ring_start(p, h):
         for u in range(2):
             hop(p, h, 1, u, True).start()
             hop(p, h, 1, 1 - u, False).start()
 
-    def ring_step(p, h, k, last=False):
+    def ring_step(p, h, k, last=False, q=None):
         for u in range(2):
             arrived(p, h, k, u, True)
             if not last or u == 0:
@@ -289,46 +313,79 @@
             arrived(p, h, k, 1 - u, False)
             if not last or u == 0:
                 hop(p, h, k + 1, 1 - u, False).start()
-        picks_at(p, h, k)
-
-    def ring_end(p, h):
+        picks_at(p, h, k, q)
+
+    def ring_end(p, h, q=None):
         arrived(p, h, Z // 2, 0, True)
         arrived(p, h, Z // 2, 1, False)
-        send_picks(p, h, (z + Z // 2) % Z)
-
-    def picks_at(p, h, k):
-        send_picks(p, h, (z - k + Z) % Z)
-        send_picks(p, h, (z + k) % Z)
-
-    def routed(p, h):
+        send_picks(p, h, (z + Z // 2) % Z, q)
+
+    def picks_at(p, h, k, q):
+        send_picks(p, h, (z - k + Z) % Z, q)
+        send_picks(p, h, (z + k) % Z, q)
+
+    def routed(p, h, q=None):
         for i in range(Y - 1):
-            wait_all(field[p][h].at[pl.ds(PLANE + i * SLOTS, SLOTS)], y_r.at[p, h, i])
-
-    def forward(p, h):
+            wait_all(slots[p][h][q or 0].at[pl.ds(i * SLOTS, SLOTS)], y_r.at[p, h, i, q or 0])
+
+    def block_of(p, h, at, q):
+        own = jnp.full((SC, BS if q is None else BS // 2), at, jnp.int32) < PLANE
+        near = field[p][h][jnp.minimum(at, PLANE - 1), :, part_of(q)]
+        return jnp.where(own, near, slots[p][h][q or 0][jnp.maximum(at - PLANE, 0)])
+
+    def forward(p, h, q=None):
+        cols = part_of(q)
+
         def tile(t):
             def one(d):
                 dest = (me + d) % C
                 at = d * TD + t
-                fsend[p][h][at] = field[p][h][meta[FWD + dest * TD + t]]
+                fsend[p][h][at, :, cols] = block_of(p, h, meta[FWD + dest * TD + t], q)
                 remote(
-                    fsend[p][h].at[at],
-                    frecv[p][h].at[t, d],
+                    fsend[p][h].at[at, :, cols],
+                    frecv[p][h].at[t, d, :, cols],
                     f_s.at[p, h],
                     f_r.at[p, h, t],
                     at_c(d),
                 ).start()
 
             each(1, C, one)
-            frecv[p][h][t, 0] = field[p][h][meta[FWD + me * TD + t]]
+            frecv[p][h][t, 0, :, cols] = block_of(p, h, meta[FWD + me * TD + t], q)
 
         each(0, TD, tile)
 
-    def forwarded(p, h, t):
-        wait_all(frecv[p][h].at[t, pl.ds(1, C - 1)], f_r.at[p, h, t])
+    def forward_half(p, h):
+        cols = part_of(0)
+
+        def one(d):
+            dest = (me + d) % C
+            for t in range(TD):
+                at = d * TD + t
+                fsend[p][h][at, :, cols] = block_of(p, h, meta[FWD + dest * TD + t], 0)
+            remote(
+                fsend[p][h].at[pl.ds(d * TD, TD), :, cols],
+                frecv[p][h].at[:, d, :, cols],
+                f_s.at[p, h],
+                f_r.at[p, h, TD],
+                at_c(d),
+            ).start()
+
+        each(1, C, one)
+        for t in range(TD):
+            frecv[p][h][t, 0, :, cols] = block_of(p, h, meta[FWD + me * TD + t], 0)
+
+    def forwarded(p, h, t, q=None):
+        wait_all(frecv[p][h].at[t, pl.ds(1, C - 1), :, part_of(q)], f_r.at[p, h, t])
+
+    def forwarded_half(p, h):
+        wait_all(frecv[p][h].at[:, pl.ds(1, C - 1), :, part_of(0)], f_r.at[p, h, TD])
 
     def products(h):
+        if h == 0:
+            forwarded_half(0, h)
+
         def one(t):
-            forwarded(0, h, t)
+            forwarded(0, h, t, 1 if h == 0 else None)
             hi, lo = split2(frecv[0][h][t].reshape(C * SC, BS))
             both = dot(jnp.concatenate([hi, lo], axis=0), tile_hi[t], ((1,), (1,)))
             value = both[: C * SC] + both[C * SC :] + dot(hi, tile_lo[t], ((1,), (1,)))
@@ -380,25 +437,31 @@
 
     scale = step_size * 0.5 / (NC * C * SC)
 
-    def gradient_step(h, finish):
+    def gradient_step(h, q=None):
+        cols = part_of(q)
+        width = BS if q is None else BS // 2
+        if q == 0:
+            forwarded_half(1, h)
+
         def one(t):
-            forwarded(1, h, t)
+            if q != 0:
+                forwarded(1, h, t, q)
             block = meta[ROWS + t]
             rows = lambda p: group[p][h][:, block].reshape(C * SC, BS)
             left_hi, left_lo = split2(jnp.concatenate([rows(1), rows(0)], axis=0))
-            right = [frecv[p][h][t].reshape(C * SC, BS) for p in range(2)]
+            right = [frecv[p][h][t, :, :, cols].reshape(C * SC, width) for p in range(2)]
             right_hi, right_lo = split2(jnp.concatenate(right, axis=0))
             left = jnp.concatenate([left_hi, left_hi, left_lo], axis=0)
             right = jnp.concatenate([right_hi, right_lo, right_hi], axis=0)
             total = dot(left, right, ((0,), (0,)))
-            stepped = tile_f32[t] - scale * total
-            if finish:
-                i = lax.broadcasted_iota(jnp.int32, (BS, BS), 0)
-                j = lax.broadcasted_iota(jnp.int32, (BS, BS), 1)
-                flag = jnp.full((BS, BS), meta[DIAG + t], jnp.int32)
+            stepped = tile_f32[t, :, cols] - scale * total
+            if q is not None:
+                i = lax.broadcasted_iota(jnp.int32, (BS, width), 0)
+                j = lax.broadcasted_iota(jnp.int32, (BS, width), 1) + q * width
+                flag = jnp.full((BS, width), meta[DIAG + t], jnp.int32)
                 stepped = jnp.where((i == j) & (flag != 0), 0.0, stepped)
-            tile_f32[t] = stepped
-            if finish:
+            tile_f32[t, :, cols] = stepped
+            if q == 1:
                 pltpu.make_async_copy(tile_f32.at[t], tiles_out.at[t], local.at[1 + t]).start()
 
         each(0, TD, one)
@@ -416,23 +479,26 @@
     far_step = Z // 2 - 1
 
     ring_start(0, 0)
-    send_picks(0, 0, z)
+    send_picks(0, 0, z, 0)
     send_picks(0, 1, z)
     each(
         1,
         C,
         lambda d: remote(part.at[2], score_c.at[d], exch_s.at[2], exch_r.at[2], at_c(d)).start(),
     )
-    each(1, far_step, lambda k: ring_step(0, 0, k))
-    ring_step(0, 0, far_step, last=True)
+    each(1, far_step, lambda k: ring_step(0, 0, k, q=0))
+    ring_step(0, 0, far_step, last=True, q=0)
     ring_start(0, 1)
     gather_pass(window_at, w_r, v_s, v_r)
-    ring_end(0, 0)
+    ring_end(0, 0, 0)
+    send_rest(0, 0)
+    routed(0, 0, 0)
+    forward_half(0, 0)
     each(1, far_step, lambda k: ring_step(0, 1, k))
-    routed(0, 0)
-    forward(0, 0)
     ring_step(0, 1, far_step, last=True)
     ring_end(0, 1)
+    routed(0, 0, 1)
+    forward(0, 0, 1)
     products(0)
     group_residual()
 
@@ -450,21 +516,25 @@
 
     apply_rows(1)
     ring_start(1, 1)
-    send_picks(1, 1, z)
+    send_picks(1, 1, z, 0)
     routed(1, 0)
     forward(1, 0)
     rows_start(1)
-    each(1, far_step, lambda k: ring_step(1, 1, k))
-    ring_step(1, 1, far_step, last=True)
-    ring_end(1, 1)
+    each(1, far_step, lambda k: ring_step(1, 1, k, q=0))
+    ring_step(1, 1, far_step, last=True, q=0)
+    ring_end(1, 1, 0)
+    send_rest(1, 1)
     rows_pass(1)
     gathered(group_at(0), h_r.at[0])
-    gradient_step(0, False)
+    gradient_step(0)
     gathered(group_at(1), h_r.at[1])
     each(0, BLK, diag_step)
-    routed(1, 1)
-    forward(1, 1)
-    gradient_step(1, True)
+    routed(1, 1, 0)
+    forward_half(1, 1)
+    gradient_step(1, 0)
+    routed(1, 1, 1)
+    forward(1, 1, 1)
+    gradient_step(1, 1)
 
     wait_all(score_z.at[pl.ds(1, Z - 1)], exch_s.at[0])
     wait_all(score_y.at[pl.ds(1, Y - 1)], exch_s.at[1])
@@ -489,8 +559,9 @@
     y, z = row // Z, row % Z
     tiles = C * TD
     of_group = lambda ids, g: lax.dynamic_slice(ids, (g * tiles,), (tiles,))
-    cols = jnp.stack([of_group(tile_cols, ((y + d) % Y) * Z + z) for d in range(Y)])
-    rows = of_group(tile_rows, row)
+    slices = [of_group(tile_cols, ((y + d) % Y) * Z + z) for d in range(Y)]
+    *slices, rows = lax.optimization_barrier((*slices, of_group(tile_rows, row)))
+    cols = jnp.stack(slices)
     source, local = cols // BLK, cols % BLK
     place = jnp.arange(tiles)
     rank = jnp.sum(
@@ -542,6 +613,7 @@
     vmem = lambda *shape: pltpu.VMEM(shape, f32)
     dma = lambda *shape: pltpu.SemaphoreType.DMA(shape)
     in_vmem = pl.BlockSpec(memory_space=pltpu.VMEM)
+    in_hbm = pl.BlockSpec(memory_space=pltpu.HBM)
     anywhere = pl.BlockSpec(memory_space=pl.ANY)
     n = 2 * NC
     new_tiles, new_diagonal = pl.pallas_call(
@@ -552,10 +624,10 @@
         ),
         in_specs=[
             pl.BlockSpec(memory_space=pltpu.SMEM),
-            in_vmem,
-            in_vmem,
-            in_vmem,
-            anywhere,
+            in_hbm,
+            in_hbm,
+            in_hbm,
+            in_hbm,
         ],
         out_specs=(anywhere, in_vmem),
         scratch_shapes=[
@@ -566,15 +638,19 @@
             vmem(C, ns, BLK * BS),
             vmem(BLK, SC, BS),
             vmem(C * TD, SC, BS),
+            vmem(ns, BLK * BS),
+            pltpu.VMEM(loadings.shape, jnp.bfloat16),
+            vmem(1, BLK * BS),
             vmem(TD, BS, BS),
             pltpu.VMEM((TD, BS, BS), jnp.bfloat16),
             pltpu.VMEM((TD, BS, BS), jnp.bfloat16),
         ]
-        + [vmem(PLANE + (Y - 1) * SLOTS, SC, BS)] * n
+        + [vmem(PLANE, SC, BS)] * n
         + [vmem((Y - 1) * SLOTS, SC, BS)] * n
         + [vmem(C * TD, SC, BS)] * n
         + [vmem(TD, C, SC, BS)] * n
         + [vmem(C, BLK, SC, BS)] * n
+        + [vmem((Y - 1) * SLOTS, SC, BS // parts) for parts in (2, 2, 1, 1, 2, 2)]
         + [vmem(C * TD, SC, BS)] * NC
         + [vmem(C * TD, SC, BS)] * NC
         + [
@@ -583,9 +659,9 @@
             dma(2, NC, 2),
             dma(2, NC, 2, Z // 2 + 1, 2),
             dma(2, NC, Y - 1),
-            dma(2, NC, Y - 1),
+            dma(2, NC, Y - 1, 2),
             dma(2, NC),
-            dma(2, NC, TD),
+            dma(2, NC, TD + 1),
             dma(NC),
             dma(NC),
             dma(NC, C // 2),
@@ -596,13 +672,19 @@
             dma(C // 2),
             dma(C // 2),
             dma(C // 2),
-            dma(1 + TD),
+            dma(4 + TD),
         ],
         compiler_params=pltpu.CompilerParams(
             collective_id=0, has_side_effects=True, vmem_limit_bytes=46 * 1024 * 1024
         ),
         name="route",
-    )(table, samples, loadings, omega_diagonal.reshape(1, BLK * BS), omega_tiles)
+    )(
+        table,
+        *(
+            pltpu.with_memory_space_constraint(x, pltpu.HBM)
+            for x in (samples, loadings, omega_diagonal.reshape(1, BLK * BS), omega_tiles)
+        ),
+    )
 
     limit = step_size * penalty
     new_tiles = new_tiles - jnp.clip(new_tiles, -limit, limit)

time: 127 us -> 133 us (1.047)
  Pallas kernels: 114 us -> 126 us
  local copies, waits for them, and re-layouts: 4.98 us -> 2.48 us
  other arithmetic: 5.75 us -> 4.19 us
    pallas_call x1, Pallas kernels: 114 us -> 126 us  [per_device(): pl.pallas_call(route_kernel, out_shape=(jax.ShapeDtypeStruct(omega_tiles....]
    unnamed x7 -> x1, local copies, waits for them, and re-layouts: 3.87 us -> 0.61 us
    dynamic_slice x0 -> x2, local copies, waits for them, and re-layouts: none -> 1.7 us  [index_table(): of_group = lambda ids, g: lax.dynamic_slice(ids, (g * tiles,), (tiles,))]
where the time goes in v5:
time: 133 us
  Pallas kernels  126 us (95%)
  other arithmetic  4.19 us (3%)
  local copies, waits for them, and re-layouts  2.48 us (2%)
    pallas_call x1, Pallas kernels, per_device(): pl.pallas_call(route_kernel, out_shape=(jax.ShapeDtypeStruct(omega_tiles....  126 us
    sub x1, other arithmetic, per_device(): new_tiles = new_tiles - jnp.clip(new_tiles, -limit, limit)  3.02 us

profile of v5, /device:TPU:1, one launch (start us, length us, event | category | flops | bytes accessed | tf_op | source)
XLA Modules:
  0.0 133.2 jit_solution(3634463915288217668)
XLA Ops:
  0.8 0.8 dynamic_slice.19
  1.6 0.9 fusion.9
  2.5 0.2 select_reduce_fusion.3
  2.7 0.1 convert_reduce_fusion.2
  2.9 0.2 fusion
  3.1 0.1 select_reduce_fusion.1
  3.2 0.2 convert_reduce_fusion
  3.5 0.2 select_reduce_fusion
  3.7 0.1 reshape.351
  3.8 0.1 concatenate.29.meta
  3.9 125.7 %route.1 = (f32[5,512,512]{2,1,0:T(8,128)S(1)}, f32[1,4096]{1,0:T(1,128)S(1)}) custom-call(s32[218]{0:T(256)S(1)} %concatenate.29.meta, f32[16,4096]{1,0:T(8,128)} %samples_in.1, bf16[256,4096]{1,0:T(8,128)(2,1)} %loadings_in.1, f32[1,4096]{1,0:T(1,128)} %bitcast.28, f32[5,512,512]{2,1,0:T(8,128)} %tiles.1), custom_call_target="tpu_custom_call" | custom-call | tf_op jit(solution)/shard_map/route/pallas_call | solution.py:619
  129.6 3.0 %clamp_subtract_fusion = f32[5,512,512]{2,1,0:T(8,128)} fusion(f32[5,512,512]{2,1,0:T(8,128)S(1)} %get-tuple-element.14), kind=kLoop, calls=%fused_computation | loop fusion | flops 2621440 | bytes 10485760 | tf_op jit(solution)/shard_map/sub | solution.py:690
  132.6 0.6 copy.9
  (14 shorter events, 0.1 us)

commit v6 on v4

--- a/solution.py
+++ b/solution.py
@@ -54,9 +54,9 @@
 
 def route_kernel(
     meta,
-    samples,
-    loadings,
-    diag,
+    samples_in,
+    loadings_in,
+    diag_in,
     tiles,
     tiles_out,
     diag_out,
@@ -67,6 +67,9 @@
     window,
     stage,
     seg,
+    samples,
+    loadings,
+    diag,
     tile_f32,
     tile_hi,
     tile_lo,
@@ -135,6 +138,14 @@
     greet(at_z, Z)
     greet(at_y, Y)
     greet(at_c, C)
+    loads = [
+        pltpu.make_async_copy(src, dst, local.at[1 + TD + i])
+        for i, (src, dst) in enumerate(
+            ((samples_in, samples), (loadings_in, loadings), (diag_in, diag))
+        )
+    ]
+    for load in loads:
+        load.start()
     tile_copy = pltpu.make_async_copy(tiles, tile_f32, local.at[0])
     tile_copy.start()
 
@@ -157,6 +168,8 @@
         cols = pl.ds(pl.multiple_of(b * BS, BS), BS)
         return total + dot(split3(samples[:, cols]), loadings[:, cols], ((1,), (1,)))
 
+    for load in loads:
+        load.wait()
     ns = NC * SC
     total = lax.fori_loop(0, BLK, score_step, jnp.zeros((3 * ns, loadings.shape[0]), jnp.float32))
     part[0] = total[:ns] + total[ns : 2 * ns] + total[2 * ns :]
@@ -489,8 +502,9 @@
     y, z = row // Z, row % Z
     tiles = C * TD
     of_group = lambda ids, g: lax.dynamic_slice(ids, (g * tiles,), (tiles,))
-    cols = jnp.stack([of_group(tile_cols, ((y + d) % Y) * Z + z) for d in range(Y)])
-    rows = of_group(tile_rows, row)
+    slices = [of_group(tile_cols, ((y + d) % Y) * Z + z) for d in range(Y)]
+    *slices, rows = lax.optimization_barrier((*slices, of_group(tile_rows, row)))
+    cols = jnp.stack(slices)
     source, local = cols // BLK, cols % BLK
     place = jnp.arange(tiles)
     rank = jnp.sum(
@@ -542,6 +556,7 @@
     vmem = lambda *shape: pltpu.VMEM(shape, f32)
     dma = lambda *shape: pltpu.SemaphoreType.DMA(shape)
     in_vmem = pl.BlockSpec(memory_space=pltpu.VMEM)
+    in_hbm = pl.BlockSpec(memory_space=pltpu.HBM)
     anywhere = pl.BlockSpec(memory_space=pl.ANY)
     n = 2 * NC
     new_tiles, new_diagonal = pl.pallas_call(
@@ -552,10 +567,10 @@
         ),
         in_specs=[
             pl.BlockSpec(memory_space=pltpu.SMEM),
-            in_vmem,
-            in_vmem,
-            in_vmem,
-            anywhere,
+            in_hbm,
+            in_hbm,
+            in_hbm,
+            in_hbm,
         ],
         out_specs=(anywhere, in_vmem),
         scratch_shapes=[
@@ -566,6 +581,9 @@
             vmem(C, ns, BLK * BS),
             vmem(BLK, SC, BS),
             vmem(C * TD, SC, BS),
+            vmem(ns, BLK * BS),
+            pltpu.VMEM(loadings.shape, jnp.bfloat16),
+            vmem(1, BLK * BS),
             vmem(TD, BS, BS),
             pltpu.VMEM((TD, BS, BS), jnp.bfloat16),
             pltpu.VMEM((TD, BS, BS), jnp.bfloat16),
@@ -596,13 +614,19 @@
             dma(C // 2),
             dma(C // 2),
             dma(C // 2),
-            dma(1 + TD),
+            dma(4 + TD),
         ],
         compiler_params=pltpu.CompilerParams(
             collective_id=0, has_side_effects=True, vmem_limit_bytes=46 * 1024 * 1024
         ),
         name="route",
-    )(table, samples, loadings, omega_diagonal.reshape(1, BLK * BS), omega_tiles)
+    )(
+        table,
+        *(
+            pltpu.with_memory_space_constraint(x, pltpu.HBM)
+            for x in (samples, loadings, omega_diagonal.reshape(1, BLK * BS), omega_tiles)
+        ),
+    )
 
     limit = step_size * penalty
     new_tiles = new_tiles - jnp.clip(new_tiles, -limit, limit)

time: 127 us -> 123 us (0.969)
  local copies, waits for them, and re-layouts: 4.98 us -> 2.48 us
  other arithmetic: 5.75 us -> 4.19 us
    unnamed x7 -> x1, local copies, waits for them, and re-layouts: 3.87 us -> 0.61 us
    dynamic_slice x0 -> x2, local copies, waits for them, and re-layouts: none -> 1.7 us  [index_table(): of_group = lambda ids, g: lax.dynamic_slice(ids, (g * tiles,), (tiles,))]
where the time goes in v6:
time: 123 us; the launch traced here: 122 us
  Pallas kernels  115 us (93%)
  other arithmetic  4.19 us (3%)
  local copies, waits for them, and re-layouts  2.48 us (2%)
    pallas_call x1, Pallas kernels, per_device(): pl.pallas_call(route_kernel, out_shape=(jax.ShapeDtypeStruct(omega_tiles....  115 us
    sub x1, other arithmetic, per_device(): new_tiles = new_tiles - jnp.clip(new_tiles, -limit, limit)  3.02 us

profile of v6, /device:TPU:1, one launch (start us, length us, event | category | flops | bytes accessed | tf_op | source)
XLA Modules:
  0.0 122.4 jit_solution(13392118958495096490)
XLA Ops:
  0.8 0.8 dynamic_slice.19
  1.6 0.9 fusion.9
  2.5 0.2 select_reduce_fusion.3
  2.7 0.1 convert_reduce_fusion.2
  2.9 0.2 fusion
  3.1 0.1 select_reduce_fusion.1
  3.2 0.2 convert_reduce_fusion
  3.5 0.2 select_reduce_fusion
  3.7 0.1 reshape.351
  3.8 0.1 concatenate.29.meta
  3.9 114.9 %route.1 = (f32[5,512,512]{2,1,0:T(8,128)S(1)}, f32[1,4096]{1,0:T(1,128)S(1)}) custom-call(s32[218]{0:T(256)S(1)} %concatenate.29.meta, f32[16,4096]{1,0:T(8,128)} %samples_in.1, bf16[256,4096]{1,0:T(8,128)(2,1)} %loadings_in.1, f32[1,4096]{1,0:T(1,128)} %bitcast.28, f32[5,512,512]{2,1,0:T(8,128)} %tiles.1), custom_call_target="tpu_custom_call" | custom-call | tf_op jit(solution)/shard_map/route/pallas_call | solution.py:562
  118.8 3.0 %clamp_subtract_fusion = f32[5,512,512]{2,1,0:T(8,128)} fusion(f32[5,512,512]{2,1,0:T(8,128)S(1)} %get-tuple-element.14), kind=kLoop, calls=%fused_computation | loop fusion | flops 2621440 | bytes 10485760 | tf_op jit(solution)/shard_map/sub | solution.py:632
  121.8 0.6 copy.9
  (14 shorter events, 0.1 us)

commit v7 on v6

--- a/solution.py
+++ b/solution.py
@@ -135,9 +135,6 @@
             ),
         )
 
-    greet(at_z, Z)
-    greet(at_y, Y)
-    greet(at_c, C)
     loads = [
         pltpu.make_async_copy(src, dst, local.at[1 + TD + i])
         for i, (src, dst) in enumerate(
@@ -146,6 +143,9 @@
     ]
     for load in loads:
         load.start()
+    greet(at_z, Z)
+    greet(at_y, Y)
+    greet(at_c, C)
     tile_copy = pltpu.make_async_copy(tiles, tile_f32, local.at[0])
     tile_copy.start()
 
@@ -207,8 +207,6 @@
         lambda d: remote(part.at[0], score_z.at[d], exch_s.at[0], exch_r.at[0], at_z(d)).start(),
     )
     gather_start(samples, window_at, w_s, w_r, v_s, v_r)
-    tile_copy.wait()
-    split_tiles(0, 12)
     wait_all(score_z.at[pl.ds(1, Z - 1)], exch_r.at[0])
     total = part[0]
     for d in range(1, Z):
@@ -219,7 +217,6 @@
         Y,
         lambda d: remote(part.at[1], score_y.at[d], exch_s.at[1], exch_r.at[1], at_y(d)).start(),
     )
-    split_tiles(12, TD * 4)
     wait_all(score_y.at[pl.ds(1, Y - 1)], exch_r.at[1])
     for d in range(1, Y):
         total = total + score_y[d]
@@ -275,7 +272,8 @@
         ref = field[p][h]
         stage[...] = ref[pl.ds(zs * BLK, BLK)]
 
-        def to_plane(i):
+        def to_plane(turn):
+            i = (turn + 1) % (Y - 1)
             base = i * SLOTS + zs * CAP
             for j in range(CAP):
                 ysend[p][h][base + j] = stage[meta[PICK + base + j]]
@@ -441,6 +439,8 @@
     ring_start(0, 1)
     gather_pass(window_at, w_r, v_s, v_r)
     ring_end(0, 0)
+    tile_copy.wait()
+    split_tiles(0, TD * 4)
     each(1, far_step, lambda k: ring_step(0, 1, k))
     routed(0, 0)
     forward(0, 0)
@@ -449,15 +449,15 @@
     products(0)
     group_residual()
 
+    routed(0, 1)
+    forward(0, 1)
     apply_rows(0)
     ring_start(1, 0)
     send_picks(1, 0, z)
-    routed(0, 1)
-    forward(0, 1)
     rows_start(0)
     each(1, far_step, lambda k: ring_step(1, 0, k))
+    products(1)
     ring_step(1, 0, far_step, last=True)
-    products(1)
     ring_end(1, 0)
     rows_pass(0)
 
@@ -503,8 +503,8 @@
     tiles = C * TD
     of_group = lambda ids, g: lax.dynamic_slice(ids, (g * tiles,), (tiles,))
     slices = [of_group(tile_cols, ((y + d) % Y) * Z + z) for d in range(Y)]
-    *slices, rows = lax.optimization_barrier((*slices, of_group(tile_rows, row)))
-    cols = jnp.stack(slices)
+    ids = lax.optimization_barrier(jnp.stack([*slices, of_group(tile_rows, row)]))
+    cols, rows = ids[:Y], ids[Y]
     source, local = cols // BLK, cols % BLK
     place = jnp.arange(tiles)
     rank = jnp.sum(

time: 123 us -> 119 us (0.967)
  Pallas kernels: 115 us -> 112 us
    pallas_call x1, Pallas kernels: 115 us -> 112 us  [per_device(): pl.pallas_call(route_kernel, out_shape=(jax.ShapeDtypeStruct(omega_tiles....]
    dynamic_slice x2 -> x0, local copies, waits for them, and re-layouts: 1.7 us -> none  [index_table(): of_group = lambda ids, g: lax.dynamic_slice(ids, (g * tiles,), (tiles,))]
where the time goes in v7:
time: 119 us
  Pallas kernels  112 us (94%)
  other arithmetic  4.2 us (4%)
  local copies, waits for them, and re-layouts  1.75 us (1%)
    pallas_call x1, Pallas kernels, per_device(): pl.pallas_call(route_kernel, out_shape=(jax.ShapeDtypeStruct(omega_tiles....  112 us
    sub x1, other arithmetic, per_device(): new_tiles = new_tiles - jnp.clip(new_tiles, -limit, limit)  3.02 us

profile of v7, /device:TPU:1, one launch (start us, length us, event | category | flops | bytes accessed | tf_op | source)
XLA Modules:
  0.0 119.1 jit_solution(6163989778644904909)
XLA Ops:
  0.8 0.9 dynamic-slice_bitcast_fusion.1
  1.8 0.2 select_reduce_fusion.3
  2.0 0.1 convert_reduce_fusion.2
  2.1 0.2 fusion
  2.3 0.1 select_reduce_fusion.1
  2.5 0.2 convert_reduce_fusion
  2.8 0.2 select_reduce_fusion
  3.0 0.1 reshape.119
  3.1 0.1 concatenate.3.meta
  3.2 112.3 %route.1 = (f32[5,512,512]{2,1,0:T(8,128)S(1)}, f32[1,4096]{1,0:T(1,128)S(1)}) custom-call(s32[218]{0:T(256)S(1)} %concatenate.3.meta, f32[16,4096]{1,0:T(8,128)} %samples_in.1, bf16[256,4096]{1,0:T(8,128)(2,1)} %loadings_in.1, f32[1,4096]{1,0:T(1,128)} %bitcast.38, f32[5,512,512]{2,1,0:T(8,128)} %tiles.1), custom_call_target="tpu_custom_call" | custom-call | tf_op jit(solution)/shard_map/route/pallas_call | solution.py:562
  115.4 3.0 %clamp_subtract_fusion = f32[5,512,512]{2,1,0:T(8,128)} fusion(f32[5,512,512]{2,1,0:T(8,128)S(1)} %get-tuple-element.4), kind=kLoop, calls=%fused_computation | loop fusion | flops 2621440 | bytes 10485760 | tf_op jit(solution)/shard_map/sub | solution.py:632
  118.4 0.6 copy.9
  (16 shorter events, 0.2 us)

commit v8 on v7

--- a/solution.py
+++ b/solution.py
@@ -455,8 +455,9 @@
     ring_start(1, 0)
     send_picks(1, 0, z)
     rows_start(0)
-    each(1, far_step, lambda k: ring_step(1, 0, k))
+    ring_step(1, 0, 1)
     products(1)
+    each(2, far_step, lambda k: ring_step(1, 0, k))
     ring_step(1, 0, far_step, last=True)
     ring_end(1, 0)
     rows_pass(0)

time: 119 us -> 120 us (level)
  no operation moved by 1% of the time
where the time goes in v8:
time: 120 us
  Pallas kernels  113 us (94%)
  other arithmetic  4.2 us (4%)
  local copies, waits for them, and re-layouts  1.75 us (1%)
    pallas_call x1, Pallas kernels, per_device(): pl.pallas_call(route_kernel, out_shape=(jax.ShapeDtypeStruct(omega_tiles....  113 us
    sub x1, other arithmetic, per_device(): new_tiles = new_tiles - jnp.clip(new_tiles, -limit, limit)  3.02 us

profile of v8, /device:TPU:1, one launch (start us, length us, event | category | flops | bytes accessed | tf_op | source)
XLA Modules:
  0.0 120.2 jit_solution(16627826284246760837)
XLA Ops:
  0.8 0.9 dynamic-slice_bitcast_fusion.1
  1.8 0.2 select_reduce_fusion.3
  2.0 0.1 convert_reduce_fusion.2
  2.1 0.2 fusion
  2.3 0.1 select_reduce_fusion.1
  2.5 0.2 convert_reduce_fusion
  2.8 0.2 select_reduce_fusion
  3.0 0.1 reshape.119
  3.1 0.1 concatenate.3.meta
  3.2 113.4 %route.1 = (f32[5,512,512]{2,1,0:T(8,128)S(1)}, f32[1,4096]{1,0:T(1,128)S(1)}) custom-call(s32[218]{0:T(256)S(1)} %concatenate.3.meta, f32[16,4096]{1,0:T(8,128)} %samples_in.1, bf16[256,4096]{1,0:T(8,128)(2,1)} %loadings_in.1, f32[1,4096]{1,0:T(1,128)} %bitcast.38, f32[5,512,512]{2,1,0:T(8,128)} %tiles.1), custom_call_target="tpu_custom_call" | custom-call | tf_op jit(solution)/shard_map/route/pallas_call | solution.py:563
  116.6 3.0 %clamp_subtract_fusion = f32[5,512,512]{2,1,0:T(8,128)} fusion(f32[5,512,512]{2,1,0:T(8,128)S(1)} %get-tuple-element.4), kind=kLoop, calls=%fused_computation | loop fusion | flops 2621440 | bytes 10485760 | tf_op jit(solution)/shard_map/sub | solution.py:633
  119.6 0.6 copy.9
  (16 shorter events, 0.2 us)
